TPU v7x, 32 devices: a whole 2x2x4 slice. The times are simulated.
32 devices in a mesh: gx: 8 (over y, x, core), gy: 4 (over z).
Axes of the slice: x: 2, y: 2, z: 4, core: 2. Of those that a mesh axis runs over, the one named last changes fastest.
Arguments:
- diffusivity: float32 [256, 512], P('gx', 'gy'), may hold values from 0.25 to 1
- base_humidity: float32 [256, 512], P('gx', 'gy'), may hold values from -4 to 4
- coupling: float32 [256, 512], P('gx', 'gy'), may hold values from 0.1 to 0.4
- basis_rows: float32 [256, 64], P('gx'), may hold values from -0.45 to 0.45
- basis_cols: float32 [512, 32], P('gy'), may hold values from -0.45 to 0.45
- directions: float32 [16, 64, 32], replicated, may hold values from -5 to 5
- send_cell: int32 [8, 4, 8, 8], P('gx', 'gy'), may hold values from 0 to 4095
- send_weight: float32 [8, 4, 8, 8], P('gx', 'gy'), may hold values from 0.1 to 1
- send_count: int32 [8, 4, 8], P('gx', 'gy'), may hold values from 1 to 8, as said below
- owner_gauge: int32 [8, 4, 8, 8], P('gx', 'gy'), may hold values from 0 to 39
- noise_precision: float32 [8, 4, 40], P('gx', 'gy'), may hold values from 1 to 16
Outputs:
- readings: float32 [8, 4, 16, 40], P('gx', 'gy')
- hess_action: float32 [16, 64, 32], replicated
Inputs may be any that keep to these rules, and one draw needn't show every extreme that they name: `send_count`: entries from one device to one owner; in every draw, in each row of the gy axis one owner receives exactly 8 from every device. `send_cell`: A local cell index of the sending device. `owner_gauge`: A gauge of the owner.
All inputs are finite; a program needn't handle non-finite values.
Results may differ from a plain program's by a relative error of at most 0.00011.
Values sent between devices are 32-bit elements; how exact they have to be, the bound alone decides.
A program may use at most 64 MiB of HBM per device.

v0:
```python
import jax
import jax.numpy as jnp
from jax import lax
from jax.sharding import PartitionSpec as P

STEPS = 6


step_ratio = 0.2
exact = lax.Precision.HIGHEST


def extended(cells, sides, width):
    for axis, dim in sides:
        count = lax.axis_size(axis)
        ends = count - 1
        head = lax.slice_in_dim(cells, 0, width, axis=dim)
        tail = lax.slice_in_dim(cells, cells.shape[dim] - width, cells.shape[dim], axis=dim)
        cells = jnp.concatenate(
            [
                lax.ppermute(tail, axis, [(i, (i + 1) % count) for i in range(ends)]),
                cells,
                lax.ppermute(head, axis, [((i + 1) % count, i) for i in range(ends)]),
            ],
            axis=dim,
        )
    return cells


def spread(field):
    middle = field[..., 1:-1, 1:-1]
    return (
        middle,
        (field[..., :-2, 1:-1], field[..., 2:, 1:-1], field[..., 1:-1, :-2], field[..., 1:-1, 2:]),
    )


def window(field, have, want):
    offset = have - want
    return field[..., offset : field.shape[-2] - offset, offset : field.shape[-1] - offset]


def advance(state_now, static_pad, orient):
    temp_mid, temp_near = spread(state_now[0])
    hum_mid, hum_near = spread(state_now[1])
    diff_mid, diff_near = spread(static_pad[0])
    couple_mid = static_pad[2, 1:-1, 1:-1]
    inside = static_pad[3, 1:-1, 1:-1]
    lap_temp = sum((n - temp_mid for n in temp_near))
    lap_hum = sum((0.5 * (diff_mid + k) * (n - hum_mid) for k, n in zip(diff_near, hum_near)))
    new_temp = temp_mid + step_ratio * lap_temp + orient * couple_mid * hum_mid
    new_hum = hum_mid + step_ratio * lap_hum - orient * couple_mid * temp_mid
    return jnp.stack([new_temp * inside, new_hum * inside])


def make_source(param_pad, static_pad):
    param_mid, param_near = spread(param_pad)
    hum_mid, hum_near = spread(static_pad[1])
    inside = static_pad[3, 1:-1, 1:-1]
    return (
        sum((0.5 * (param_mid + p) * (h - hum_mid) for p, h in zip(param_near, hum_near))) * inside
    )


def state_rim(state_now):
    return extended(state_now, (("gx", 2), ("gy", 3)), 1)


def local(
    diffusivity,
    base_humidity,
    coupling,
    basis_rows,
    basis_cols,
    directions,
    send_cell,
    send_weight,
    send_count,
    owner_gauge,
    noise_precision,
):
    rim_depth = STEPS
    height, breadth = diffusivity.shape
    n_dirs = directions.shape[0]
    static = jnp.stack([diffusivity, base_humidity, coupling, jnp.ones_like(diffusivity)])
    static_wide = extended(static, (("gx", 1), ("gy", 2)), rim_depth)
    static_near = window(static_wide, rim_depth, 1)
    perturb = jnp.einsum("xa,rab->rxb", basis_rows, directions, precision=exact)
    perturb = jnp.einsum("rxb,yb->rxy", perturb, basis_cols, precision=exact)
    param_field = diffusivity * perturb
    param_wide = extended(param_field, (("gx", 1), ("gy", 2)), 1)
    source = make_source(param_wide, static_near)
    state_now = jnp.stack([jnp.zeros_like(source), step_ratio * source])
    for i in range(rim_depth - 1):
        state_now = advance(state_rim(state_now), static_near, 1.0)
        state_now = jnp.stack([state_now[0], state_now[1] + step_ratio * source])
    humid = state_now[1]
    peers = send_cell.shape[2]
    slots = send_cell.shape[3]
    gauges = noise_precision.shape[2]
    cell_ids = send_cell.reshape(-1)
    live_mask = (
        lax.broadcasted_iota(jnp.int32, (peers, slots), 1) < send_count.reshape(peers, 1)
    ).astype(jnp.float32)
    factor = send_weight.reshape(peers, slots) * live_mask
    picked = (
        jnp.take(humid.reshape(n_dirs, height * breadth), cell_ids, axis=1).reshape(
            n_dirs, peers, slots
        )
        * factor
    )
    gauge_ids = owner_gauge.reshape(-1)
    lookup = (gauge_ids[:, None] == lax.broadcasted_iota(jnp.int32, (1, gauges), 1)).astype(
        jnp.float32
    )
    gauge_weights = noise_precision.reshape(1, gauges)
    arrived = lax.all_to_all(picked, "gx", split_axis=1, concat_axis=1, tiled=True)
    n_items = arrived.shape[0]
    gauge_read = jnp.dot(arrived.reshape(n_items, peers * slots), lookup, precision=exact)
    backward = jnp.dot(gauge_read * gauge_weights, lookup.T, precision=exact).reshape(
        n_items, peers, slots
    )
    returned = lax.all_to_all(backward, "gx", split_axis=1, concat_axis=1, tiled=True)
    gauge_read, returned = (gauge_read, returned)
    load_values = (returned * factor).reshape(n_dirs, peers * slots)
    adjoint_load = (
        jnp.zeros((n_dirs, height * breadth), jnp.float32).at[:, cell_ids].add(load_values)
    )
    adjoint_load = adjoint_load.reshape(n_dirs, height, breadth)
    state_now = jnp.stack([jnp.zeros_like(adjoint_load), adjoint_load])
    summed = adjoint_load
    for i in range(rim_depth - 1):
        state_now = advance(state_rim(state_now), static_near, -1.0)
        summed = summed + state_now[1]
    lam_wide = extended(step_ratio * summed, (("gx", 1), ("gy", 2)), 1)
    lam_mid, lam_near = spread(lam_wide)
    hum_mid, hum_near = spread(static_near[1])
    gradient = diffusivity * sum(
        (0.5 * (h - hum_mid) * (lam_mid - l) for h, l in zip(hum_near, lam_near))
    )
    projected = jnp.einsum("rxy,yb->rxb", gradient, basis_cols, precision=exact)
    projected = jnp.einsum("xa,rxb->rab", basis_rows, projected, precision=exact).reshape(
        n_dirs, -1
    )
    summed_modes = lax.psum(projected, ("gx", "gy"))
    hess_action = directions + summed_modes.reshape(directions.shape)
    return (gauge_read.reshape(1, 1, n_dirs, gauges), hess_action)


def solution(mesh):
    placed = (
        P("gx", "gy"),
        P("gx", "gy"),
        P("gx", "gy"),
        P("gx", None),
        P("gy", None),
        P(),
        P("gx", "gy", None, None),
        P("gx", "gy", None, None),
        P("gx", "gy", None),
        P("gx", "gy", None, None),
        P("gx", "gy", None),
    )
    return jax.shard_map(
        local,
        mesh=mesh,
        in_specs=placed,
        out_specs=(P("gx", "gy", None, None), P()),
        check_vma=False,
    )
```

profile of v0, /device:TPU:0, one launch (start us, length us, event | category | flops | bytes accessed | tf_op | source)
XLA Modules:
  0.0 442.1 jit_solution(16900153259718897505)
XLA Ops:
  9.9 2.4 collective-permute-start
  14.3 5.1 %collective-permute-start.1 = (f32[4,6,128]{2,1,0:T(8,128)S(1)}, f32[4,6,128]{2,1,0:T(8,128)S(1)}, u32[]{:S(2)}, u32[]{:S(2)}) collective-permute-start(f32[4,6,128]{2,1,0:T(8,128)S(1)} %get-tuple-element.90), channel_id=1, source_target_pairs={{0,4},{4,8},{8,12},{12,16},{16,20},{20,24},{24,28},{1,5},{5,9},{9,... | collective-permute-start | bytes 36872 | tf_op jit(solution)/shard_map/ppermute | solution.py:21
  20.9 2.9 collective-permute-done.2
  23.9 3.5 collective-permute-start.3
  28.9 4.6 %collective-permute-start.6 = (f32[16,34,1]{2,1,0:T(8,128)S(1)}, f32[16,34,1]{2,1,0:T(8,128)S(1)}, u32[]{:S(2)}, u32[]{:S(2)}) collective-permute-start(f32[16,34,1]{2,1,0:T(8,128)S(1)} %get-tuple-element.76), channel_id=1, source_target_pairs={{0,1},{1,2},{2,3},{4,5},{5,6},{6,7},{8,9},{9,10},{10,11},{12,13},{... | collective-permute-start | bytes 6536 | tf_op jit(solution)/shard_map/ppermute | solution.py:21
  35.2 5.4 %collective-permute-done.6 = f32[16,34,1]{2,1,0:T(8,128)S(1)} collective-permute-done((f32[16,34,1]{2,1,0:T(8,128)S(1)}, f32[16,34,1]{2,1,0:T(8,128)S(1)}, u32[]{:S(2)}, u32[]{:S(2)}) %collective-permute-start.6) | collective-permute-done | bytes 2208 | tf_op jit(solution)/shard_map/ppermute | solution.py:21
  40.6 4.7 %collective-permute-done.7 = f32[16,34,1]{2,1,0:T(8,128)S(1)} collective-permute-done((f32[16,34,1]{2,1,0:T(8,128)S(1)}, f32[16,34,1]{2,1,0:T(8,128)S(1)}, u32[]{:S(2)}, u32[]{:S(2)}) %collective-permute-start.7) | collective-permute-done | bytes 2208 | tf_op jit(solution)/shard_map/ppermute | solution.py:23
  45.7 2.3 collective-permute-start.8
  53.9 4.5 %collective-permute-start.10 = (f32[2,16,34,1]{2,1,3,0:T(8,128)S(1)}, f32[2,16,34,1]{2,1,3,0:T(8,128)S(1)}, u32[]{:S(2)}, u32[]{:S(2)}) collective-permute-start(f32[2,16,34,1]{2,1,3,0:T(8,128)S(1)} %copy.23), channel_id=1, source_target_pairs={{0,1},{1,2},{2,3},{4,5},{5,6},{6,7},{8,9},{9,10},{10,11},{12,13},{... | collective-permute-start | bytes 13064 | tf_op jit(solution)/shard_map/ppermute | solution.py:21
  62.3 3.2 collective-permute-start.12
  66.9 2.9 collective-permute-done.13
  70.4 4.2 collective-permute-start.14
  76.6 4.0 collective-permute-done.15
  82.6 3.2 collective-permute-start.16
  87.1 3.4 collective-permute-done.17
  91.2 3.5 collective-permute-start.18
  96.6 4.0 collective-permute-done.19
  102.7 3.2 collective-permute-start.20
  107.2 3.3 collective-permute-done.21
  112.8 4.5 %collective-permute-start.22 = (f32[2,16,34,1]{2,1,3,0:T(8,128)S(1)}, f32[2,16,34,1]{2,1,3,0:T(8,128)S(1)}, u32[]{:S(2)}, u32[]{:S(2)}) collective-permute-start(f32[2,16,34,1]{2,1,3,0:T(8,128)S(1)} %copy.35), channel_id=1, source_target_pairs={{0,1},{1,2},{2,3},{4,5},{5,6},{6,7},{8,9},{9,10},{10,11},{12,13},{... | collective-permute-start | bytes 13064 | tf_op jit(solution)/shard_map/ppermute | solution.py:21
  121.2 3.5 collective-permute-start.24
  126.0 3.1 collective-permute-done.25
  131.4 4.8 %collective-permute-start.26 = (f32[2,16,34,1]{2,1,3,0:T(8,128)S(1)}, f32[2,16,34,1]{2,1,3,0:T(8,128)S(1)}, u32[]{:S(2)}, u32[]{:S(2)}) collective-permute-start(f32[2,16,34,1]{2,1,3,0:T(8,128)S(1)} %copy.39), channel_id=1, source_target_pairs={{0,1},{1,2},{2,3},{4,5},{5,6},{6,7},{8,9},{9,10},{10,11},{12,13},{... | collective-permute-start | bytes 13064 | tf_op jit(solution)/shard_map/ppermute | solution.py:21
  141.9 6.7 %all-to-all-start = ((f32[8,1,128]{2,1,0:T(1,128)}), f32[8,1,128]{2,1,0:T(1,128)S(1)}, u32[]{:S(2)}, u32[]{:S(2)}) async-start(f32[8,1,128]{2,1,0:T(1,128)} %reshape.148), calls=%async_computation | async-start | bytes 8192 | tf_op jit(solution)/shard_map/all_to_all | solution.py:117
  148.7 4.5 %all-to-all-done = f32[8,1,128]{2,1,0:T(1,128)S(1)} async-done(((f32[8,1,128]{2,1,0:T(1,128)}), f32[8,1,128]{2,1,0:T(1,128)S(1)}, u32[]{:S(2)}, u32[]{:S(2)}) %all-to-all-start) | async-done | bytes 4128 | tf_op jit(solution)/shard_map/all_to_all | solution.py:117
  155.0 7.0 %all_to_all.10 = f32[8,1,128]{2,1,0:T(1,128)S(1)} all-to-all(f32[8,1,128]{2,1,0:T(1,128)S(1)} %reshape.150), channel_id=1, replica_groups=mesh['gx'=8,'gy'=4] {'gx'}, dimensions={0} | all-to-all | bytes 8192 | tf_op jit(solution)/shard_map/all_to_all | solution.py:123
  174.1 4.5 %collective-permute-start.30 = (f32[2,16,34,1]{2,1,3,0:T(8,128)S(1)}, f32[2,16,34,1]{2,1,3,0:T(8,128)S(1)}, u32[]{:S(2)}, u32[]{:S(2)}) collective-permute-start(f32[2,16,34,1]{2,1,3,0:T(8,128)S(1)} %copy.47), channel_id=1, source_target_pairs={{0,1},{1,2},{2,3},{4,5},{5,6},{6,7},{8,9},{9,10},{10,11},{12,13},{... | collective-permute-start | bytes 13064 | tf_op jit(solution)/shard_map/ppermute | solution.py:21
  184.2 3.5 collective-permute-start.32
  193.8 4.2 collective-permute-start.34
  200.2 3.8 collective-permute-done.35
  207.7 3.2 collective-permute-start.36
  212.2 2.4 collective-permute-done.37
  218.5 4.5 %collective-permute-start.38 = (f32[2,16,34,1]{2,1,3,0:T(8,128)}, f32[2,16,34,1]{2,1,3,0:T(8,128)}, u32[]{:S(2)}, u32[]{:S(2)}) collective-permute-start(f32[2,16,34,1]{2,1,3,0:T(8,128)} %copy.55), channel_id=1, source_target_pairs={{0,1},{1,2},{2,3},{4,5},{5,6},{6,7},{8,9},{9,10},{10,11},{12,13},{... | collective-permute-start | bytes 13064 | tf_op jit(solution)/shard_map/ppermute | solution.py:21
  226.2 3.6 collective-permute-done.39
  235.0 3.4 collective-permute-start.40
  239.7 3.1 collective-permute-done.41
  245.6 3.3 collective-permute-start.42
  252.8 3.1 collective-permute-done.43
  259.9 3.2 collective-permute-start.44
  264.3 3.4 collective-permute-done.45
  270.5 2.5 collective-permute-start.46
  278.7 2.3 collective-permute-done.47
  284.2 3.5 collective-permute-start.48
  289.0 3.0 collective-permute-done.49
  292.3 2.3 collective-permute-start.50
  296.1 4.0 collective-permute-done.50
  300.1 4.8 %collective-permute-done.51 = f32[16,34,1]{2,1,0:T(8,128)S(1)} collective-permute-done((f32[16,34,1]{2,1,0:T(8,128)S(1)}, f32[16,34,1]{2,1,0:T(8,128)S(1)}, u32[]{:S(2)}, u32[]{:S(2)}) %collective-permute-start.51) | collective-permute-done | bytes 2208 | tf_op jit(solution)/shard_map/ppermute | solution.py:23
  307.4 126.1 %all-reduce.4.cloned.1.call-done = f32[16,64,32]{1,2,0:T(8,128)} async-done(((f32[16,64,32]{1,2,0:T(8,128)}), f32[16,64,32]{1,2,0:T(8,128)}) %all-reduce.4.cloned.1.call-update) | async-done | bytes 131088 | tf_op jit(solution)/shard_map/psum | solution.py:145
  (274 shorter events, 124.1 us)
Async XLA Ops:
  9.9 10.9 %collective-permute-start = (f32[16,1,128]{2,1,0:T(1,128)S(1)}, f32[16,1,128]{2,1,0:T(1,128)S(1)}, u32[]{:S(2)}, u32[]{:S(2)}) collective-permute-start(f32[16,1,128]{2,1,0:T(1,128)S(1)} %get-tuple-element.84), channel_id=1, source_target_pairs={{0,4},{4,8},{8,12},{12,16},{16,20},{20,24},{24,28},{1,5},{5,9},{9,... | collective-permute-start | bytes 24584 | tf_op jit(solution)/shard_map/ppermute | solution.py:21
  12.3 8.5 %collective-permute-start.5 = (f32[16,1,128]{2,1,0:T(1,128)S(1)}, f32[16,1,128]{2,1,0:T(1,128)S(1)}, u32[]{:S(2)}, u32[]{:S(2)}) collective-permute-start(f32[16,1,128]{2,1,0:T(1,128)S(1)} %get-tuple-element.85), channel_id=1, source_target_pairs={{4,0},{8,4},{12,8},{16,12},{20,16},{24,20},{28,24},{5,1},{9,5},{13... | collective-permute-start | bytes 24584 | tf_op jit(solution)/shard_map/ppermute | solution.py:23
  14.3 6.5 %collective-permute-start.1 = (f32[4,6,128]{2,1,0:T(8,128)S(1)}, f32[4,6,128]{2,1,0:T(8,128)S(1)}, u32[]{:S(2)}, u32[]{:S(2)}) collective-permute-start(f32[4,6,128]{2,1,0:T(8,128)S(1)} %get-tuple-element.90), channel_id=1, source_target_pairs={{0,4},{4,8},{8,12},{12,16},{16,20},{20,24},{24,28},{1,5},{5,9},{9,... | collective-permute-start | bytes 36872 | tf_op jit(solution)/shard_map/ppermute | solution.py:21
  19.5 4.3 collective-permute-start.2
  23.9 10.8 %collective-permute-start.3 = (f32[4,44,6]{2,1,0:T(8,128)S(1)}, f32[4,44,6]{2,1,0:T(8,128)S(1)}, u32[]{:S(2)}, u32[]{:S(2)}) collective-permute-start(f32[4,44,6]{2,1,0:T(8,128)S(1)} %get-tuple-element.88), channel_id=1, source_target_pairs={{0,1},{1,2},{2,3},{4,5},{5,6},{6,7},{8,9},{9,10},{10,11},{12,13},{... | collective-permute-start | bytes 12680 | tf_op jit(solution)/shard_map/ppermute | solution.py:21
  27.4 7.3 %collective-permute-start.4 = (f32[4,44,6]{2,1,0:T(8,128)S(1)}, f32[4,44,6]{2,1,0:T(8,128)S(1)}, u32[]{:S(2)}, u32[]{:S(2)}) collective-permute-start(f32[4,44,6]{2,1,0:T(8,128)S(1)} %get-tuple-element.89), channel_id=1, source_target_pairs={{1,0},{2,1},{3,2},{5,4},{6,5},{7,6},{9,8},{10,9},{11,10},{13,12},{... | collective-permute-start | bytes 12680 | tf_op jit(solution)/shard_map/ppermute | solution.py:23
  28.9 11.7 %collective-permute-start.6 = (f32[16,34,1]{2,1,0:T(8,128)S(1)}, f32[16,34,1]{2,1,0:T(8,128)S(1)}, u32[]{:S(2)}, u32[]{:S(2)}) collective-permute-start(f32[16,34,1]{2,1,0:T(8,128)S(1)} %get-tuple-element.76), channel_id=1, source_target_pairs={{0,1},{1,2},{2,3},{4,5},{5,6},{6,7},{8,9},{9,10},{10,11},{12,13},{... | collective-permute-start | bytes 6536 | tf_op jit(solution)/shard_map/ppermute | solution.py:21
  33.4 11.9 %collective-permute-start.7 = (f32[16,34,1]{2,1,0:T(8,128)S(1)}, f32[16,34,1]{2,1,0:T(8,128)S(1)}, u32[]{:S(2)}, u32[]{:S(2)}) collective-permute-start(f32[16,34,1]{2,1,0:T(8,128)S(1)} %get-tuple-element.77), channel_id=1, source_target_pairs={{1,0},{2,1},{3,2},{5,4},{6,5},{7,6},{9,8},{10,9},{11,10},{13,12},{... | collective-permute-start | bytes 6536 | tf_op jit(solution)/shard_map/ppermute | solution.py:23
  52.6 7.6 %collective-permute-start.11 = (f32[2,16,34,1]{2,1,3,0:T(8,128)S(1)}, f32[2,16,34,1]{2,1,3,0:T(8,128)S(1)}, u32[]{:S(2)}, u32[]{:S(2)}) collective-permute-start(f32[2,16,34,1]{2,1,3,0:T(8,128)S(1)} %copy.24), channel_id=1, source_target_pairs={{1,0},{2,1},{3,2},{5,4},{6,5},{7,6},{9,8},{10,9},{11,10},{13,12},{... | collective-permute-start | bytes 13064 | tf_op jit(solution)/shard_map/ppermute | solution.py:23
  53.9 6.0 %collective-permute-start.10 = (f32[2,16,34,1]{2,1,3,0:T(8,128)S(1)}, f32[2,16,34,1]{2,1,3,0:T(8,128)S(1)}, u32[]{:S(2)}, u32[]{:S(2)}) collective-permute-start(f32[2,16,34,1]{2,1,3,0:T(8,128)S(1)} %copy.23), channel_id=1, source_target_pairs={{0,1},{1,2},{2,3},{4,5},{5,6},{6,7},{8,9},{9,10},{10,11},{12,13},{... | collective-permute-start | bytes 13064 | tf_op jit(solution)/shard_map/ppermute | solution.py:21
  62.3 4.6 %collective-permute-start.12 = (f32[2,16,1,128]{3,2,1,0:T(1,128)S(1)}, f32[2,16,1,128]{3,2,1,0:T(1,128)S(1)}, u32[]{:S(2)}, u32[]{:S(2)}) collective-permute-start(f32[2,16,1,128]{3,2,1,0:T(1,128)S(1)} %get-tuple-element.72), channel_id=1, source_target_pairs={{0,4},{4,8},{8,12},{12,16},{16,20},{20,24},{24,28},{1,5},{5,9},{9,... | collective-permute-start | bytes 49160 | tf_op jit(solution)/shard_map/ppermute | solution.py:21
  65.6 4.3 collective-permute-start.13
  70.4 5.8 %collective-permute-start.14 = (f32[2,16,34,1]{2,1,3,0:T(8,128)S(1)}, f32[2,16,34,1]{2,1,3,0:T(8,128)S(1)}, u32[]{:S(2)}, u32[]{:S(2)}) collective-permute-start(f32[2,16,34,1]{2,1,3,0:T(8,128)S(1)} %copy.27), channel_id=1, source_target_pairs={{0,1},{1,2},{2,3},{4,5},{5,6},{6,7},{8,9},{9,10},{10,11},{12,13},{... | collective-permute-start | bytes 13064 | tf_op jit(solution)/shard_map/ppermute | solution.py:21
  75.0 5.6 %collective-permute-start.15 = (f32[2,16,34,1]{2,1,3,0:T(8,128)S(1)}, f32[2,16,34,1]{2,1,3,0:T(8,128)S(1)}, u32[]{:S(2)}, u32[]{:S(2)}) collective-permute-start(f32[2,16,34,1]{2,1,3,0:T(8,128)S(1)} %copy.28), channel_id=1, source_target_pairs={{1,0},{2,1},{3,2},{5,4},{6,5},{7,6},{9,8},{10,9},{11,10},{13,12},{... | collective-permute-start | bytes 13064 | tf_op jit(solution)/shard_map/ppermute | solution.py:23
  82.6 4.5 %collective-permute-start.16 = (f32[2,16,1,128]{3,2,1,0:T(1,128)S(1)}, f32[2,16,1,128]{3,2,1,0:T(1,128)S(1)}, u32[]{:S(2)}, u32[]{:S(2)}) collective-permute-start(f32[2,16,1,128]{3,2,1,0:T(1,128)S(1)} %get-tuple-element.70), channel_id=1, source_target_pairs={{0,4},{4,8},{8,12},{12,16},{16,20},{20,24},{24,28},{1,5},{5,9},{9,... | collective-permute-start | bytes 49160 | tf_op jit(solution)/shard_map/ppermute | solution.py:21
  85.8 4.7 %collective-permute-start.17 = (f32[2,16,1,128]{3,2,1,0:T(1,128)S(1)}, f32[2,16,1,128]{3,2,1,0:T(1,128)S(1)}, u32[]{:S(2)}, u32[]{:S(2)}) collective-permute-start(f32[2,16,1,128]{3,2,1,0:T(1,128)S(1)} %get-tuple-element.71), channel_id=1, source_target_pairs={{4,0},{8,4},{12,8},{16,12},{20,16},{24,20},{28,24},{5,1},{9,5},{13... | collective-permute-start | bytes 49160 | tf_op jit(solution)/shard_map/ppermute | solution.py:23
  91.2 5.1 %collective-permute-start.18 = (f32[2,16,34,1]{2,1,3,0:T(8,128)S(1)}, f32[2,16,34,1]{2,1,3,0:T(8,128)S(1)}, u32[]{:S(2)}, u32[]{:S(2)}) collective-permute-start(f32[2,16,34,1]{2,1,3,0:T(8,128)S(1)} %copy.31), channel_id=1, source_target_pairs={{0,1},{1,2},{2,3},{4,5},{5,6},{6,7},{8,9},{9,10},{10,11},{12,13},{... | collective-permute-start | bytes 13064 | tf_op jit(solution)/shard_map/ppermute | solution.py:21
  95.0 5.6 %collective-permute-start.19 = (f32[2,16,34,1]{2,1,3,0:T(8,128)S(1)}, f32[2,16,34,1]{2,1,3,0:T(8,128)S(1)}, u32[]{:S(2)}, u32[]{:S(2)}) collective-permute-start(f32[2,16,34,1]{2,1,3,0:T(8,128)S(1)} %copy.32), channel_id=1, source_target_pairs={{1,0},{2,1},{3,2},{5,4},{6,5},{7,6},{9,8},{10,9},{11,10},{13,12},{... | collective-permute-start | bytes 13064 | tf_op jit(solution)/shard_map/ppermute | solution.py:23
  102.7 4.6 %collective-permute-start.20 = (f32[2,16,1,128]{3,2,1,0:T(1,128)S(1)}, f32[2,16,1,128]{3,2,1,0:T(1,128)S(1)}, u32[]{:S(2)}, u32[]{:S(2)}) collective-permute-start(f32[2,16,1,128]{3,2,1,0:T(1,128)S(1)} %get-tuple-element.68), channel_id=1, source_target_pairs={{0,4},{4,8},{8,12},{12,16},{16,20},{20,24},{24,28},{1,5},{5,9},{9,... | collective-permute-start | bytes 49160 | tf_op jit(solution)/shard_map/ppermute | solution.py:21
  105.8 4.7 %collective-permute-start.21 = (f32[2,16,1,128]{3,2,1,0:T(1,128)S(1)}, f32[2,16,1,128]{3,2,1,0:T(1,128)S(1)}, u32[]{:S(2)}, u32[]{:S(2)}) collective-permute-start(f32[2,16,1,128]{3,2,1,0:T(1,128)S(1)} %get-tuple-element.69), channel_id=1, source_target_pairs={{4,0},{8,4},{12,8},{16,12},{20,16},{24,20},{28,24},{5,1},{9,5},{13... | collective-permute-start | bytes 49160 | tf_op jit(solution)/shard_map/ppermute | solution.py:23
  111.5 7.6 %collective-permute-start.23 = (f32[2,16,34,1]{2,1,3,0:T(8,128)S(1)}, f32[2,16,34,1]{2,1,3,0:T(8,128)S(1)}, u32[]{:S(2)}, u32[]{:S(2)}) collective-permute-start(f32[2,16,34,1]{2,1,3,0:T(8,128)S(1)} %copy.36), channel_id=1, source_target_pairs={{1,0},{2,1},{3,2},{5,4},{6,5},{7,6},{9,8},{10,9},{11,10},{13,12},{... | collective-permute-start | bytes 13064 | tf_op jit(solution)/shard_map/ppermute | solution.py:23
  112.8 6.0 %collective-permute-start.22 = (f32[2,16,34,1]{2,1,3,0:T(8,128)S(1)}, f32[2,16,34,1]{2,1,3,0:T(8,128)S(1)}, u32[]{:S(2)}, u32[]{:S(2)}) collective-permute-start(f32[2,16,34,1]{2,1,3,0:T(8,128)S(1)} %copy.35), channel_id=1, source_target_pairs={{0,1},{1,2},{2,3},{4,5},{5,6},{6,7},{8,9},{9,10},{10,11},{12,13},{... | collective-permute-start | bytes 13064 | tf_op jit(solution)/shard_map/ppermute | solution.py:21
  121.2 4.8 %collective-permute-start.24 = (f32[2,16,1,128]{3,2,1,0:T(1,128)S(1)}, f32[2,16,1,128]{3,2,1,0:T(1,128)S(1)}, u32[]{:S(2)}, u32[]{:S(2)}) collective-permute-start(f32[2,16,1,128]{3,2,1,0:T(1,128)S(1)} %get-tuple-element.66), channel_id=1, source_target_pairs={{0,4},{4,8},{8,12},{12,16},{16,20},{20,24},{24,28},{1,5},{5,9},{9,... | collective-permute-start | bytes 49160 | tf_op jit(solution)/shard_map/ppermute | solution.py:21
  124.7 4.4 %collective-permute-start.25 = (f32[2,16,1,128]{3,2,1,0:T(1,128)S(1)}, f32[2,16,1,128]{3,2,1,0:T(1,128)S(1)}, u32[]{:S(2)}, u32[]{:S(2)}) collective-permute-start(f32[2,16,1,128]{3,2,1,0:T(1,128)S(1)} %get-tuple-element.67), channel_id=1, source_target_pairs={{4,0},{8,4},{12,8},{16,12},{20,16},{24,20},{28,24},{5,1},{9,5},{13... | collective-permute-start | bytes 49160 | tf_op jit(solution)/shard_map/ppermute | solution.py:23
  130.1 7.9 %collective-permute-start.27 = (f32[2,16,34,1]{2,1,3,0:T(8,128)S(1)}, f32[2,16,34,1]{2,1,3,0:T(8,128)S(1)}, u32[]{:S(2)}, u32[]{:S(2)}) collective-permute-start(f32[2,16,34,1]{2,1,3,0:T(8,128)S(1)} %copy.40), channel_id=1, source_target_pairs={{1,0},{2,1},{3,2},{5,4},{6,5},{7,6},{9,8},{10,9},{11,10},{13,12},{... | collective-permute-start | bytes 13064 | tf_op jit(solution)/shard_map/ppermute | solution.py:23
  131.4 6.3 %collective-permute-start.26 = (f32[2,16,34,1]{2,1,3,0:T(8,128)S(1)}, f32[2,16,34,1]{2,1,3,0:T(8,128)S(1)}, u32[]{:S(2)}, u32[]{:S(2)}) collective-permute-start(f32[2,16,34,1]{2,1,3,0:T(8,128)S(1)} %copy.39), channel_id=1, source_target_pairs={{0,1},{1,2},{2,3},{4,5},{5,6},{6,7},{8,9},{9,10},{10,11},{12,13},{... | collective-permute-start | bytes 13064 | tf_op jit(solution)/shard_map/ppermute | solution.py:21
  141.9 11.3 %all-to-all-start = ((f32[8,1,128]{2,1,0:T(1,128)}), f32[8,1,128]{2,1,0:T(1,128)S(1)}, u32[]{:S(2)}, u32[]{:S(2)}) async-start(f32[8,1,128]{2,1,0:T(1,128)} %reshape.148), calls=%async_computation | async-start | bytes 8192 | tf_op jit(solution)/shard_map/all_to_all | solution.py:117
  148.6 285.0 %all-reduce.4.cloned.1.call-start = ((), (), s32[]{:S(2)}) async-start(), calls=%async_computation.2 | async-start | bytes 524288 | tf_op jit(solution)/shard_map/psum | solution.py:145
  172.8 7.6 %collective-permute-start.31 = (f32[2,16,34,1]{2,1,3,0:T(8,128)S(1)}, f32[2,16,34,1]{2,1,3,0:T(8,128)S(1)}, u32[]{:S(2)}, u32[]{:S(2)}) collective-permute-start(f32[2,16,34,1]{2,1,3,0:T(8,128)S(1)} %copy.48), channel_id=1, source_target_pairs={{1,0},{2,1},{3,2},{5,4},{6,5},{7,6},{9,8},{10,9},{11,10},{13,12},{... | collective-permute-start | bytes 13064 | tf_op jit(solution)/shard_map/ppermute | solution.py:23
  174.1 6.0 %collective-permute-start.30 = (f32[2,16,34,1]{2,1,3,0:T(8,128)S(1)}, f32[2,16,34,1]{2,1,3,0:T(8,128)S(1)}, u32[]{:S(2)}, u32[]{:S(2)}) collective-permute-start(f32[2,16,34,1]{2,1,3,0:T(8,128)S(1)} %copy.47), channel_id=1, source_target_pairs={{0,1},{1,2},{2,3},{4,5},{5,6},{6,7},{8,9},{9,10},{10,11},{12,13},{... | collective-permute-start | bytes 13064 | tf_op jit(solution)/shard_map/ppermute | solution.py:21
  184.2 4.8 %collective-permute-start.32 = (f32[2,16,1,128]{3,2,1,0:T(1,128)S(1)}, f32[2,16,1,128]{3,2,1,0:T(1,128)S(1)}, u32[]{:S(2)}, u32[]{:S(2)}) collective-permute-start(f32[2,16,1,128]{3,2,1,0:T(1,128)S(1)} %get-tuple-element.64), channel_id=1, source_target_pairs={{0,4},{4,8},{8,12},{12,16},{16,20},{20,24},{24,28},{1,5},{5,9},{9,... | collective-permute-start | bytes 49160 | tf_op jit(solution)/shard_map/ppermute | solution.py:21
  193.8 6.0 %collective-permute-start.34 = (f32[2,16,34,1]{2,1,3,0:T(8,128)S(1)}, f32[2,16,34,1]{2,1,3,0:T(8,128)S(1)}, u32[]{:S(2)}, u32[]{:S(2)}) collective-permute-start(f32[2,16,34,1]{2,1,3,0:T(8,128)S(1)} %copy.51), channel_id=1, source_target_pairs={{0,1},{1,2},{2,3},{4,5},{5,6},{6,7},{8,9},{9,10},{10,11},{12,13},{... | collective-permute-start | bytes 13064 | tf_op jit(solution)/shard_map/ppermute | solution.py:21
  198.3 5.6 %collective-permute-start.35 = (f32[2,16,34,1]{2,1,3,0:T(8,128)S(1)}, f32[2,16,34,1]{2,1,3,0:T(8,128)S(1)}, u32[]{:S(2)}, u32[]{:S(2)}) collective-permute-start(f32[2,16,34,1]{2,1,3,0:T(8,128)S(1)} %copy.52), channel_id=1, source_target_pairs={{1,0},{2,1},{3,2},{5,4},{6,5},{7,6},{9,8},{10,9},{11,10},{13,12},{... | collective-permute-start | bytes 13064 | tf_op jit(solution)/shard_map/ppermute | solution.py:23
  207.7 4.5 %collective-permute-start.36 = (f32[2,16,1,128]{3,2,1,0:T(1,128)S(1)}, f32[2,16,1,128]{3,2,1,0:T(1,128)S(1)}, u32[]{:S(2)}, u32[]{:S(2)}) collective-permute-start(f32[2,16,1,128]{3,2,1,0:T(1,128)S(1)} %get-tuple-element.62), channel_id=1, source_target_pairs={{0,4},{4,8},{8,12},{12,16},{16,20},{20,24},{24,28},{1,5},{5,9},{9,... | collective-permute-start | bytes 49160 | tf_op jit(solution)/shard_map/ppermute | solution.py:21
  218.5 6.7 %collective-permute-start.38 = (f32[2,16,34,1]{2,1,3,0:T(8,128)}, f32[2,16,34,1]{2,1,3,0:T(8,128)}, u32[]{:S(2)}, u32[]{:S(2)}) collective-permute-start(f32[2,16,34,1]{2,1,3,0:T(8,128)} %copy.55), channel_id=1, source_target_pairs={{0,1},{1,2},{2,3},{4,5},{5,6},{6,7},{8,9},{9,10},{10,11},{12,13},{... | collective-permute-start | bytes 13064 | tf_op jit(solution)/shard_map/ppermute | solution.py:21
  223.9 5.9 %collective-permute-start.39 = (f32[2,16,34,1]{2,1,3,0:T(8,128)}, f32[2,16,34,1]{2,1,3,0:T(8,128)}, u32[]{:S(2)}, u32[]{:S(2)}) collective-permute-start(f32[2,16,34,1]{2,1,3,0:T(8,128)} %copy.56), channel_id=1, source_target_pairs={{1,0},{2,1},{3,2},{5,4},{6,5},{7,6},{9,8},{10,9},{11,10},{13,12},{... | collective-permute-start | bytes 13064 | tf_op jit(solution)/shard_map/ppermute | solution.py:23
  235.0 4.7 %collective-permute-start.40 = (f32[2,16,1,128]{3,2,1,0:T(1,128)S(1)}, f32[2,16,1,128]{3,2,1,0:T(1,128)S(1)}, u32[]{:S(2)}, u32[]{:S(2)}) collective-permute-start(f32[2,16,1,128]{3,2,1,0:T(1,128)S(1)} %get-tuple-element.60), channel_id=1, source_target_pairs={{0,4},{4,8},{8,12},{12,16},{16,20},{20,24},{24,28},{1,5},{5,9},{9,... | collective-permute-start | bytes 49160 | tf_op jit(solution)/shard_map/ppermute | solution.py:21
  238.4 4.5 %collective-permute-start.41 = (f32[2,16,1,128]{3,2,1,0:T(1,128)S(1)}, f32[2,16,1,128]{3,2,1,0:T(1,128)S(1)}, u32[]{:S(2)}, u32[]{:S(2)}) collective-permute-start(f32[2,16,1,128]{3,2,1,0:T(1,128)S(1)} %get-tuple-element.61), channel_id=1, source_target_pairs={{4,0},{8,4},{12,8},{16,12},{20,16},{24,20},{28,24},{5,1},{9,5},{13... | collective-permute-start | bytes 49160 | tf_op jit(solution)/shard_map/ppermute | solution.py:23
  245.6 6.0 %collective-permute-start.42 = (f32[2,16,34,1]{2,1,3,0:T(8,128)S(1)}, f32[2,16,34,1]{2,1,3,0:T(8,128)S(1)}, u32[]{:S(2)}, u32[]{:S(2)}) collective-permute-start(f32[2,16,34,1]{2,1,3,0:T(8,128)S(1)} %copy.59), channel_id=1, source_target_pairs={{0,1},{1,2},{2,3},{4,5},{5,6},{6,7},{8,9},{9,10},{10,11},{12,13},{... | collective-permute-start | bytes 13064 | tf_op jit(solution)/shard_map/ppermute | solution.py:21
  250.3 5.6 %collective-permute-start.43 = (f32[2,16,34,1]{2,1,3,0:T(8,128)S(1)}, f32[2,16,34,1]{2,1,3,0:T(8,128)S(1)}, u32[]{:S(2)}, u32[]{:S(2)}) collective-permute-start(f32[2,16,34,1]{2,1,3,0:T(8,128)S(1)} %copy.60), channel_id=1, source_target_pairs={{1,0},{2,1},{3,2},{5,4},{6,5},{7,6},{9,8},{10,9},{11,10},{13,12},{... | collective-permute-start | bytes 13064 | tf_op jit(solution)/shard_map/ppermute | solution.py:23
  259.9 4.5 %collective-permute-start.44 = (f32[2,16,1,128]{3,2,1,0:T(1,128)S(1)}, f32[2,16,1,128]{3,2,1,0:T(1,128)S(1)}, u32[]{:S(2)}, u32[]{:S(2)}) collective-permute-start(f32[2,16,1,128]{3,2,1,0:T(1,128)S(1)} %get-tuple-element.58), channel_id=1, source_target_pairs={{0,4},{4,8},{8,12},{12,16},{16,20},{20,24},{24,28},{1,5},{5,9},{9,... | collective-permute-start | bytes 49160 | tf_op jit(solution)/shard_map/ppermute | solution.py:21
  263.0 4.7 %collective-permute-start.45 = (f32[2,16,1,128]{3,2,1,0:T(1,128)S(1)}, f32[2,16,1,128]{3,2,1,0:T(1,128)S(1)}, u32[]{:S(2)}, u32[]{:S(2)}) collective-permute-start(f32[2,16,1,128]{3,2,1,0:T(1,128)S(1)} %get-tuple-element.59), channel_id=1, source_target_pairs={{4,0},{8,4},{12,8},{16,12},{20,16},{24,20},{28,24},{5,1},{9,5},{13... | collective-permute-start | bytes 49160 | tf_op jit(solution)/shard_map/ppermute | solution.py:23
  270.5 7.1 %collective-permute-start.46 = (f32[2,16,34,1]{2,1,3,0:T(8,128)S(1)}, f32[2,16,34,1]{2,1,3,0:T(8,128)}, u32[]{:S(2)}, u32[]{:S(2)}) collective-permute-start(f32[2,16,34,1]{2,1,3,0:T(8,128)S(1)} %copy.63), channel_id=1, source_target_pairs={{0,1},{1,2},{2,3},{4,5},{5,6},{6,7},{8,9},{9,10},{10,11},{12,13},{... | collective-permute-start | bytes 13064 | tf_op jit(solution)/shard_map/ppermute | solution.py:21
  275.0 5.9 %collective-permute-start.47 = (f32[2,16,34,1]{2,1,3,0:T(8,128)}, f32[2,16,34,1]{2,1,3,0:T(8,128)}, u32[]{:S(2)}, u32[]{:S(2)}) collective-permute-start(f32[2,16,34,1]{2,1,3,0:T(8,128)} %copy.64), channel_id=1, source_target_pairs={{1,0},{2,1},{3,2},{5,4},{6,5},{7,6},{9,8},{10,9},{11,10},{13,12},{... | collective-permute-start | bytes 13064 | tf_op jit(solution)/shard_map/ppermute | solution.py:23
  284.2 4.8 %collective-permute-start.48 = (f32[16,1,128]{2,1,0:T(1,128)S(1)}, f32[16,1,128]{2,1,0:T(1,128)S(1)}, u32[]{:S(2)}, u32[]{:S(2)}) collective-permute-start(f32[16,1,128]{2,1,0:T(1,128)S(1)} %get-tuple-element.78), channel_id=1, source_target_pairs={{0,4},{4,8},{8,12},{12,16},{16,20},{20,24},{24,28},{1,5},{5,9},{9,... | collective-permute-start | bytes 24584 | tf_op jit(solution)/shard_map/ppermute | solution.py:21
  287.7 4.4 collective-permute-start.49
  292.3 7.8 %collective-permute-start.50 = (f32[16,34,1]{2,1,0:T(8,128)S(1)}, f32[16,34,1]{2,1,0:T(8,128)S(1)}, u32[]{:S(2)}, u32[]{:S(2)}) collective-permute-start(f32[16,34,1]{2,1,0:T(8,128)S(1)} %get-tuple-element.74), channel_id=1, source_target_pairs={{0,1},{1,2},{2,3},{4,5},{5,6},{6,7},{8,9},{9,10},{10,11},{12,13},{... | collective-permute-start | bytes 6536 | tf_op jit(solution)/shard_map/ppermute | solution.py:21
  294.6 10.3 %collective-permute-start.51 = (f32[16,34,1]{2,1,0:T(8,128)S(1)}, f32[16,34,1]{2,1,0:T(8,128)S(1)}, u32[]{:S(2)}, u32[]{:S(2)}) collective-permute-start(f32[16,34,1]{2,1,0:T(8,128)S(1)} %get-tuple-element.75), channel_id=1, source_target_pairs={{1,0},{2,1},{3,2},{5,4},{6,5},{7,6},{9,8},{10,9},{11,10},{13,12},{... | collective-permute-start | bytes 6536 | tf_op jit(solution)/shard_map/ppermute | solution.py:23
  (40 other events, 1426.1 us)
Sparse Core Ops, SparseCore 0:
  307.6 125.9 all-reduce.3
where the time goes:
time: 445 us; the launch traced here: 442 us
  waiting for transfers between devices  210 us (47%)
  starting transfers between devices  133 us (30%)
  local copies, waits for them, and re-layouts  45.1 us (10%)
  other arithmetic  25.9 us (6%)
  between operations  15.5 us (3%)
  blocking collectives  7.02 us (2%)
  matrix products  5.51 us (1%)
    psum x1, waiting for transfers between devices, local(): summed_modes = lax.psum(projected, ('gx', 'gy'))  126 us
    ppermute x26, starting transfers between devices, extended(): lax.ppermute(tail, axis, [(i, (i + 1) % count) for i in range(ends)])  92.4 us
    ppermute x26, waiting for transfers between devices, extended(): lax.ppermute(head, axis, [((i + 1) % count, i) for i in range(ends)])  64.5 us
    ppermute x26, starting transfers between devices, extended(): lax.ppermute(head, axis, [((i + 1) % count, i) for i in range(ends)])  33.9 us
    slice x27, local copies, waits for them, and re-layouts, extended(): lax.slice_in_dim(cells, cells.shape[dim] - width, cells.shape[dim], axis=...  16.5 us
    ppermute x26, waiting for transfers between devices, extended(): lax.ppermute(tail, axis, [(i, (i + 1) % count) for i in range(ends)])  14.9 us
    concatenate x24, other arithmetic, extended(): jnp.concatenate([lax.ppermute(tail, axis, [(i, (i + 1) % count) for i in...  12.7 us
  transfers between devices with their start and end apart: 54, of which 28 were waited for; matrix products, arithmetic and copies ran while one was open for 3% of the time, Pallas kernels for 0%

commit v1 on v0

v1 whole, which is shorter than its diff:
```python
import functools

import jax
import jax.numpy as jnp
from jax import lax
from jax.experimental import pallas as pl
from jax.experimental.pallas import tpu as pltpu
from jax.sharding import PartitionSpec as P

STEPS = 6
step_ratio = 0.2
exact = lax.Precision.HIGHEST
f32 = jnp.float32
bf16 = jnp.bfloat16
PAD = 8
NN = (((1,), (0,)), ((), ()))
NT = (((1,), (1,)), ((), ()))


def iota(shape, dim):
    return lax.broadcasted_iota(jnp.int32, shape, dim)


def dot(a, b, dims=NN):
    return lax.dot_general(a, b, dims, precision=exact, preferred_element_type=f32)


def pick_dot(values, hot, dims=NN):
    hot = hot.astype(bf16)
    total = None
    for _ in range(3):
        part = values.astype(bf16)
        values = values - part.astype(f32)
        term = lax.dot_general(part, hot, dims, preferred_element_type=f32)
        total = term if total is None else total + term
    return total


def around(v):
    rows, cols = v.shape
    return (
        pltpu.roll(v, 1, 0),
        pltpu.roll(v, rows - 1, 0),
        pltpu.roll(v, 1, 1),
        pltpu.roll(v, cols - 1, 1),
    )


def turned(v):
    rows, cols = v.shape
    if cols % 128:
        v = jnp.concatenate([v, jnp.zeros((rows, 128 - cols % 128), f32)], axis=1)
    if rows % 128:
        v = jnp.concatenate([v, jnp.zeros((128 - rows % 128, v.shape[1]), f32)], axis=0)
    return v.T


def column(row):
    m = row.shape[1]
    same = iota((m, m), 0) == iota((m, m), 1)
    return jnp.sum(jnp.where(same, jnp.broadcast_to(row, (m, m)), 0.0), axis=1, keepdims=True)


def flat_row(x, first, width):
    peers, slots = x.shape
    lane = iota((slots, width), 1)
    hot = (lane % slots == iota((slots, width), 0)).astype(f32)
    wide = pick_dot(x, hot)
    mine = (iota((peers, width), 1) + first) // slots == iota((peers, width), 0)
    return jnp.sum(jnp.where(mine, wide, 0.0), axis=0, keepdims=True)


def slot_of(dx, dy):
    return (dx + 1) * 3 + dy + 1


def kernel(
    n_gx, n_gy,
    diff_ref, base_ref, couple_ref, rows_ref, cols_ref, dirs_ref,
    cell_ref, weight_ref, count_ref, gauge_ref, prec_ref,
    read_ref, hess_ref,
    pc, pt, pb, rc, rr, coef, gcoef, first_sc, pert, hum, pk, qb, rb, vr, load, grad,
    proj, rsb, agb,
    near_send, near_recv, own_send, own_recv, back_send, back_recv,
    rs_send, rs_recv, ag_send, ag_recv,
):
    gx, gy = lax.axis_index("gx"), lax.axis_index("gy")
    n = n_gx * n_gy
    me = gx * n_gy + gy
    height, breadth = diff_ref.shape
    n_dirs, modes_x, modes_y = dirs_ref.shape
    peers, slots = cell_ref.shape[2], cell_ref.shape[3]
    gauges = prec_ref.shape[2]
    entries = peers * slots
    width = min(entries, 128)
    chunks = entries // width
    ext = height + 2 * PAD
    half = breadth // 2
    meta_c, meta_r = 3 * height + modes_y, 4 * PAD

    rc[...] = jnp.zeros_like(rc)
    rr[...] = jnp.zeros_like(rr)
    vr[...] = jnp.zeros_like(vr)

    barrier = pltpu.get_barrier_semaphore()

    def greet(i, carry):
        t = lax.rem(me + i, n)
        pl.semaphore_signal(
            barrier, inc=1, device_id=(t // n_gy, lax.rem(t, n_gy)),
            device_id_type=pl.DeviceIdType.MESH,
        )
        return carry

    lax.fori_loop(1, n, greet, 0)

    live = iota((peers, slots), 1).astype(f32) < column(count_ref[0].astype(f32))
    factor = jnp.where(live, weight_ref[0, 0], 0.0)
    cells = cell_ref[0, 0]
    cell_x, cell_y = (cells // breadth).astype(f32), (cells % breadth).astype(f32)
    pt[...] = jnp.zeros_like(pt)
    pb[...] = jnp.zeros_like(pb)
    pc[meta_c : meta_c + 8, :] = jnp.zeros((8, breadth), f32)
    my_rows = []
    for c in range(chunks):
        trio = [flat_row(v, c * width, width) for v in (cell_x, cell_y, factor)]
        my_rows.append(trio)
        for k, row in enumerate(trio):
            at = 2 * k + c
            pc[meta_c + at : meta_c + at + 1, :width] = row
            pt[meta_r + at : meta_r + at + 1, :width] = row
            pb[meta_r + at : meta_r + at + 1, :width] = row
    for k, ref in enumerate((diff_ref, base_ref, couple_ref)):
        pc[k * height : (k + 1) * height, :] = ref[...]
        pt[k * PAD : (k + 1) * PAD, :] = ref[:PAD, :]
        pb[k * PAD : (k + 1) * PAD, :] = ref[height - PAD :, :]
    pt[3 * PAD : 4 * PAD, :modes_x] = rows_ref[:PAD, :]
    pb[3 * PAD : 4 * PAD, :modes_x] = rows_ref[height - PAD :, :]
    cols_t = turned(cols_ref[...])[:modes_y]
    pc[3 * height : 3 * height + modes_y, :] = cols_t

    pl.semaphore_wait(barrier, n - 1)

    def exists(dx, dy):
        ok = None
        for d, at, size in ((dx, gx, n_gx), (dy, gy, n_gy)):
            if d:
                here = at > 0 if d < 0 else at < size - 1
                ok = here if ok is None else jnp.logical_and(ok, here)
        return ok

    def near_ref(dx, dy):
        if dx == 0:
            return rc.at[(dy + 1) // 2]
        return rr.at[(dx + 1) // 2 * 3 + dy + 1]

    def near_copy(dx, dy):
        src = pc if dx == 0 else (pt if dx < 0 else pb)
        return pltpu.make_async_remote_copy(
            src_ref=src, dst_ref=near_ref(-dx, -dy),
            send_sem=near_send.at[slot_of(dx, dy)], recv_sem=near_recv.at[slot_of(-dx, -dy)],
            device_id=(gx + dx, gy + dy), device_id_type=pl.DeviceIdType.MESH,
        )

    sides = [(dx, dy) for dx in (0, -1, 1) for dy in (-1, 0, 1) if dx or dy]
    for dx, dy in sides:

        @pl.when(exists(dx, dy))
        def _(dx=dx, dy=dy):
            near_copy(dx, dy).start()

    for dx, dy in sides:

        @pl.when(exists(dx, dy))
        def _(dx=dx, dy=dy):
            near_copy(-dx, -dy).wait_recv()

    lane = iota((ext, breadth), 1)

    def joined(middle, right, left):
        return jnp.concatenate([middle, jnp.where(iota(right.shape, 1) < half, right, left)], axis=1)

    def extended(k, ref):
        tile = slice(k * PAD, (k + 1) * PAD)
        block = slice(k * height, (k + 1) * height)
        stack = lambda dy, mid: jnp.concatenate(
            [rr[dy + 1, tile, :], mid, rr[3 + dy + 1, tile, :]], axis=0
        )
        return joined(stack(0, ref[...]), stack(1, rc[1, block, :]), stack(-1, rc[0, block, :]))

    diff = extended(0, diff_ref)
    base = extended(1, base_ref)
    couple = extended(2, couple_ref)
    row_at, lane_at = iota((ext, 2 * breadth), 0), iota((ext, 2 * breadth), 1)
    out_row = jnp.logical_or(
        jnp.logical_and(row_at < PAD, gx == 0),
        jnp.logical_and(row_at >= PAD + height, gx == n_gx - 1),
    )
    out_col = jnp.logical_or(
        jnp.logical_and(
            jnp.logical_and(lane_at >= breadth, lane_at < breadth + half), gy == n_gy - 1
        ),
        jnp.logical_and(lane_at >= breadth + half, gy == 0),
    )
    inside = jnp.where(jnp.logical_or(out_row, out_col), 0.0, 1.0).astype(f32)
    centre = inside
    s_sum = jnp.zeros_like(diff)
    own = (slice(PAD, PAD + height), slice(0, breadth))
    for k, (d_near, b_near) in enumerate(zip(around(diff), around(base))):
        weight = (step_ratio * 0.5) * (diff + d_near) * inside
        coef[1 + k] = weight
        centre = centre - weight
        gap = 0.5 * (b_near - base)
        gcoef[k] = (diff * gap)[own]
        pull = step_ratio * gap * inside
        coef[9 + k] = pull
        s_sum = s_sum + pull
    coef[0] = centre
    coef[5] = step_ratio * inside
    coef[6] = couple
    coef[7] = diff
    coef[8] = s_sum

    rows_ext = jnp.concatenate(
        [rr[1, 3 * PAD : 4 * PAD, :modes_x], rows_ref[...], rr[4, 3 * PAD : 4 * PAD, :modes_x]],
        axis=0,
    )
    own_cols = slice(3 * height, 3 * height + modes_y)
    cols_ext = joined(cols_t, rc[1, own_cols, :], rc[0, own_cols, :])
    for r in range(n_dirs):
        first_sc[r * ext : (r + 1) * ext, :] = dot(rows_ext, dirs_ref[r])
    pert[...] = dot(first_sc[...], cols_ext).reshape(n_dirs, ext, 2 * breadth)

    def stencil(t, h, sign):
        t_near, h_near = around(t), around(h)
        mixed = coef[0] * h
        total = t
        for k in range(4):
            mixed = mixed + coef[1 + k] * h_near[k]
            total = total + t_near[k]
        if sign > 0:
            return coef[5] * total + coef[6] * h, mixed - coef[6] * t
        return coef[5] * total - coef[6] * h, mixed + coef[6] * t

    def tangent(r, carry):
        p = coef[7] * pert[r]
        source = coef[8] * p
        for k, p_near in enumerate(around(p)):
            source = source + coef[9 + k] * p_near
        t, h = coef[6] * source, coef[0] * source
        for k, s_near in enumerate(around(source)):
            h = h + coef[1 + k] * s_near
        h = h + source
        for _ in range(STEPS - 2):
            t, h = stencil(t, h, 1)
            h = h + source
        hum[r] = h[own]
        return carry

    lax.fori_loop(0, n_dirs, tangent, 0)

    humid = hum[...].reshape(n_dirs * height, breadth)
    for c in range(chunks):
        x_row, y_row, f_row = my_rows[c]
        hot = (iota((breadth, width), 0).astype(f32) == y_row).astype(f32)
        picked = pick_dot(humid, hot).reshape(n_dirs, height, width)
        mine = jnp.where(iota((height, width), 0).astype(f32) == x_row, f_row, 0.0)
        picked = jnp.sum(picked * mine[None], axis=1)
        some = width // slots
        pk[c * some : (c + 1) * some] = turned(picked)[:width].reshape(some, slots, 128)

    def to_owner(o, slot):
        return pltpu.make_async_remote_copy(
            src_ref=pk.at[o], dst_ref=qb.at[slot], send_sem=own_send, recv_sem=own_recv,
            device_id=(o, gy), device_id_type=pl.DeviceIdType.MESH,
        )

    def send_picks(i, carry):
        to_owner(lax.rem(gx + i, n_gx), gx).start()
        return carry

    lax.fori_loop(1, n_gx, send_picks, 0)
    qb[gx] = pk[gx]
    gauge_f = gauge_ref[0, 0].astype(f32)
    hots = []
    for c in range(chunks):
        g_row = flat_row(gauge_f, c * width, width)
        hots.append((iota((128, width), 0).astype(f32) == g_row).astype(f32))
    prec = column(prec_ref[0])
    prec = jnp.concatenate([prec, jnp.zeros((128 - gauges, 1), f32)], axis=0)
    others = pl.ds(0, n_gx - 1)
    everyone = pltpu.make_async_remote_copy(
        src_ref=pk.at[others], dst_ref=qb.at[others], send_sem=own_send, recv_sem=own_recv,
        device_id=(gx, gy), device_id_type=pl.DeviceIdType.MESH,
    )
    everyone.wait_recv()
    some = width // slots
    gauge_read = jnp.zeros((128, 128), f32)
    for c in range(chunks):
        got = qb[c * some : (c + 1) * some].reshape(width, 128)
        gauge_read = gauge_read + dot(hots[c], got)
    weighted = gauge_read * prec
    rb[0] = jnp.zeros((slots, 128), f32)
    rb[n_gx + 1] = jnp.zeros((slots, 128), f32)
    for c in range(chunks):
        back = dot(turned(hots[c])[:width], weighted)
        rb[1 + c * some : 1 + (c + 1) * some] = back.reshape(some, slots, 128)

    def back_copy(t, dy):
        return pltpu.make_async_remote_copy(
            src_ref=rb.at[pl.ds(t, 3)], dst_ref=vr.at[1 - dy, :, gx],
            send_sem=back_send.at[1 + dy], recv_sem=back_recv.at[1 - dy],
            device_id=(t, gy + dy), device_id_type=pl.DeviceIdType.MESH,
        )

    def send_back(i, carry):
        t = lax.rem(gx + i, n_gx)
        for dy in (-1, 1):

            @pl.when(exists(0, dy))
            def _(dy=dy):
                back_copy(t, dy).start()

        @pl.when(i > 0)
        def _():
            back_copy(t, 0).start()

        return carry

    lax.fori_loop(0, n_gx, send_back, 0)
    vr[1, :, gx] = rb[pl.ds(gx, 3)]
    read_ref[0, 0] = gauge_read.T[:n_dirs, :gauges]

    def back_all(dy):
        span = pl.ds(0, n_gx if dy else n_gx - 1)
        return pltpu.make_async_remote_copy(
            src_ref=vr.at[1 + dy, :, span], dst_ref=vr.at[1 + dy, :, span],
            send_sem=back_send.at[1 + dy], recv_sem=back_recv.at[1 + dy],
            device_id=(gx, gy), device_id_type=pl.DeviceIdType.MESH,
        )

    back_all(0).wait_recv()
    for dy in (-1, 1):

        @pl.when(exists(0, dy))
        def _(dy=dy):
            back_all(dy).wait_recv()

    def meta_row(dx, dy, k, c):
        if dx == 0 and dy == 0:
            return my_rows[c][k]
        at = 2 * k + c
        if dx == 0:
            return rc[(dy + 1) // 2, meta_c + at : meta_c + at + 1, :width]
        return rr[(dx + 1) // 2 * 3 + dy + 1, meta_r + at : meta_r + at + 1, :width]

    for dx, at, first, tall in ((-1, 0, height - PAD, PAD), (0, PAD, 0, height), (1, PAD + height, 0, PAD)):
        parts = [None, None]
        for dy in (-1, 0, 1):
            for c in range(chunks):
                x_row, y_row, f_row = (meta_row(dx, dy, k, c) for k in range(3))
                got = vr[dy + 1, dx + 1, c * some : (c + 1) * some].reshape(width, 128)
                values = turned(got)[:n_dirs, :width] * f_row
                hit_x = (iota((tall, width), 0) + first).astype(f32) == x_row
                y_at = iota((breadth, width), 0)
                hit_y = y_at.astype(f32) == y_row
                if dy:
                    hit_y = jnp.logical_and(hit_y, y_at < half if dy > 0 else y_at >= half)
                spread_x = jnp.where(hit_x[None], values[:, None, :], 0.0)
                term = pick_dot(
                    spread_x.reshape(n_dirs * tall, width), hit_y.astype(f32), NT
                )
                tile = 1 if dy else 0
                parts[tile] = term if parts[tile] is None else parts[tile] + term
        for tile in (0, 1):
            load[:, at : at + tall, tile * breadth : (tile + 1) * breadth] = parts[tile].reshape(
                n_dirs, tall, breadth
            )

    group = 128 // modes_y

    def adjoint(r, carry):
        b = load[r]
        summed = b
        a, b = -(coef[6] * b), coef[0] * b
        for k, l_near in enumerate(around(summed)):
            b = b + coef[1 + k] * l_near
        summed = summed + b
        for _ in range(STEPS - 2):
            a, b = stencil(a, b, -1)
            summed = summed + b
        lam = step_ratio * summed
        total = None
        for k, l_near in enumerate(around(lam)):
            term = gcoef[k] * (lam[own] - l_near[own])
            total = term if total is None else total + term
        grad[lax.rem(r, group), r // group] = total
        return carry

    lax.fori_loop(0, n_dirs, adjoint, 0)

    quads = n_dirs // group
    half_way = None
    for j in range(group):
        pieces = []
        if j:
            pieces.append(jnp.zeros((j * modes_y, breadth), f32))
        pieces.append(cols_t)
        if j < group - 1:
            pieces.append(jnp.zeros(((group - 1 - j) * modes_y, breadth), f32))
        placed = jnp.concatenate(pieces, axis=0)
        term = dot(grad[j].reshape(quads * height, breadth), placed, NT)
        half_way = term if half_way is None else half_way + term
    rows_t = turned(rows_ref[...])[:modes_x, :height]
    size = proj.shape[1]
    per = modes_x // size
    for q in range(quads):
        both = dot(rows_t, half_way[q * height : (q + 1) * height])
        if per:
            proj[q * per : (q + 1) * per] = both.reshape(per, size, 128)
        else:
            ratio = size // modes_x
            proj[q // ratio, (q % ratio) * modes_x : (q % ratio + 1) * modes_x] = both

    owners = proj.shape[0]

    def share(t):
        return pltpu.make_async_remote_copy(
            src_ref=proj.at[t], dst_ref=rsb.at[me], send_sem=rs_send, recv_sem=rs_recv,
            device_id=(t // n_gy, lax.rem(t, n_gy)), device_id_type=pl.DeviceIdType.MESH,
        )

    def result(t):
        return pltpu.make_async_remote_copy(
            src_ref=agb.at[me], dst_ref=agb.at[me], send_sem=ag_send, recv_sem=ag_recv,
            device_id=(t // n_gy, lax.rem(t, n_gy)), device_id_type=pl.DeviceIdType.MESH,
        )

    def waiter(ref, count, send, recv):
        span = ref.at[pl.ds(0, count)]
        return pltpu.make_async_remote_copy(
            src_ref=span, dst_ref=span, send_sem=send, recv_sem=recv,
            device_id=(gx, gy), device_id_type=pl.DeviceIdType.MESH,
        )

    def send_share(i, carry):
        t = lax.rem(me + i, n)
        if owners == n:
            share(t).start()
        else:

            @pl.when(t < owners)
            def _():
                share(t).start()

        return carry

    lax.fori_loop(1, n, send_share, 0)

    def own_part():
        rsb[me] = proj[me]
        waiter(rsb, n - 1, rs_send, rs_recv).wait_recv()
        agb[me] = jnp.sum(rsb[...], axis=0)

        def send_result(i, carry):
            result(lax.rem(me + i, n)).start()
            return carry

        lax.fori_loop(1, n, send_result, 0)
        if owners > 1:
            waiter(agb, owners - 1, ag_send, ag_recv).wait_recv()
        waiter(rsb, n - 1, ag_send, ag_recv).wait_send()
        if owners > 1:
            waiter(agb, owners - 1, rs_send, rs_recv).wait_send()

    def other_part():
        waiter(agb, owners, ag_send, ag_recv).wait_recv()
        waiter(agb, owners, rs_send, rs_recv).wait_send()

    if owners == n:
        own_part()
    else:
        pl.when(me < owners)(own_part)
        pl.when(me >= owners)(other_part)

    summed = agb[...].reshape(quads, modes_x, 128)
    for r in range(n_dirs):
        q, j = r // group, r % group
        hess_ref[r] = dirs_ref[r] + summed[q][:, j * modes_y : (j + 1) * modes_y]

    for dx, dy in sides:

        @pl.when(exists(dx, dy))
        def _(dx=dx, dy=dy):
            near_copy(dx, dy).wait_send()

    everyone.wait_send()
    back_all(0).wait_send()
    for dy in (-1, 1):

        @pl.when(exists(0, dy))
        def _(dy=dy):
            back_all(dy).wait_send()


def local(n_gx, n_gy, *args):
    diffusivity, dirs, cells, noise = args[0], args[5], args[6], args[10]
    height, breadth = diffusivity.shape
    n_dirs, modes_x, modes_y = dirs.shape
    peers, slots = cells.shape[2], cells.shape[3]
    gauges = noise.shape[2]
    n = n_gx * n_gy
    ext = height + 2 * PAD
    total_rows = n_dirs * modes_x * modes_y // 128
    size = max(8, total_rows // n)
    owners = total_rows // size
    group = 128 // modes_y
    vmem = lambda *shape: pltpu.VMEM(shape, f32)
    dma = pltpu.SemaphoreType.DMA
    space = pl.BlockSpec(memory_space=pltpu.VMEM)
    return pl.pallas_call(
        functools.partial(kernel, n_gx, n_gy),
        out_shape=(
            jax.ShapeDtypeStruct((1, 1, n_dirs, gauges), f32),
            jax.ShapeDtypeStruct(dirs.shape, f32),
        ),
        in_specs=[space] * len(args),
        out_specs=(space, space),
        scratch_shapes=[
            vmem(3 * height + modes_y + 8, breadth),
            vmem(5 * PAD, breadth),
            vmem(5 * PAD, breadth),
            vmem(2, 3 * height + modes_y + 8, breadth),
            vmem(6, 5 * PAD, breadth),
            vmem(13, ext, 2 * breadth),
            vmem(4, height, breadth),
            vmem(n_dirs * ext, modes_y),
            vmem(n_dirs, ext, 2 * breadth),
            vmem(n_dirs, height, breadth),
            vmem(peers, slots, 128),
            vmem(peers, slots, 128),
            vmem(peers + 2, slots, 128),
            vmem(3, 3, peers, slots, 128),
            vmem(n_dirs, ext, 2 * breadth),
            vmem(group, n_dirs // group, height, breadth),
            vmem(owners, size, 128),
            vmem(n, size, 128),
            vmem(owners, size, 128),
            dma((9,)),
            dma((9,)),
            dma,
            dma,
            dma((3,)),
            dma((3,)),
            dma,
            dma,
            dma,
            dma,
        ],
        compiler_params=pltpu.CompilerParams(
            collective_id=0, has_side_effects=True, vmem_limit_bytes=40 * 1024 * 1024
        ),
    )(*args)


def solution(mesh):
    placed = (
        P("gx", "gy"),
        P("gx", "gy"),
        P("gx", "gy"),
        P("gx", None),
        P("gy", None),
        P(),
        P("gx", "gy", None, None),
        P("gx", "gy", None, None),
        P("gx", "gy", None),
        P("gx", "gy", None, None),
        P("gx", "gy", None),
    )
    return jax.shard_map(
        functools.partial(local, mesh.shape["gx"], mesh.shape["gy"]),
        mesh=mesh,
        in_specs=placed,
        out_specs=(P("gx", "gy", None, None), P()),
        check_vma=False,
    )
```

time: 445 us -> 57.5 us (0.13)
  waiting for transfers between devices: 210 us -> 0 us
  starting transfers between devices: 133 us -> 0 us
  Pallas kernels: 0 us -> 52.9 us
  local copies, waits for them, and re-layouts: 45.1 us -> 3.56 us
  other arithmetic: 25.9 us -> 0 us
  between operations: 15.5 us -> 0.79 us
  blocking collectives: 7.02 us -> 0 us
  matrix products: 5.51 us -> 0 us
    ppermute x52 -> x0, starting transfers between devices: 126 us -> none  [the longest x26 92.4 us: extended(): lax.ppermute(tail, axis, [(i, (i + 1) % count) for i in range(ends)])]
    psum x1 -> x0, waiting for transfers between devices: 126 us -> none  [local(): summed_modes = lax.psum(projected, ('gx', 'gy'))]
    ppermute x52 -> x0, waiting for transfers between devices: 79.5 us -> none  [the longest x26 64.5 us: extended(): lax.ppermute(head, axis, [((i + 1) % count, i) for i in range(ends)])]
    pallas_call x0 -> x1, Pallas kernels: none -> 52.9 us  [local(): pl.pallas_call(functools.partial(kernel, n_gx, n_gy), out_shape=(jax.Shap...]
    slice x37 -> x0, local copies, waits for them, and re-layouts: 23.1 us -> none  [the longest x27 16.5 us: extended(): lax.slice_in_dim(cells, cells.shape[dim] - width, cells.shape[dim], axis=...]
    ppermute x20 -> x0, local copies, waits for them, and re-layouts: 14 us -> none  [the longest x10 8.26 us: extended(): lax.ppermute(head, axis, [((i + 1) % count, i) for i in range(ends)])]
    concatenate x24 -> x0, other arithmetic: 12.7 us -> none  [extended(): jnp.concatenate([lax.ppermute(tail, axis, [(i, (i + 1) % count) for i in...]
    all_to_all x1 -> x0, blocking collectives: 7.02 us -> none  [local(): lax.all_to_all(backward, 'gx', split_axis=1, concat_axis=1, tiled=True)]
  transfers between devices with their start and end apart: 54 -> 0, of which waited for: 28 -> 0; matrix products, arithmetic and copies ran while one was open for 3% -> 0% of each run, Pallas kernels for 0% -> 0%
where the time goes in v1:
time: 57.5 us; the launch traced here: 57.3 us
  Pallas kernels  52.9 us (92%)
  local copies, waits for them, and re-layouts  3.56 us (6%)
  between operations  0.79 us (1%)
    pallas_call x1, Pallas kernels, local(): pl.pallas_call(functools.partial(kernel, n_gx, n_gy), out_shape=(jax.Shap...  52.9 us
    unnamed x21, local copies, waits for them, and re-layouts  2.66 us

profile of v1, /device:TPU:0, one launch (start us, length us, event | category | flops | bytes accessed | tf_op | source)
XLA Modules:
  0.0 57.3 jit_solution(17062723921784362652)
XLA Ops:
  0.6 0.8 %copy.13.cols_ref = f32[128,32]{1,0:T(8,128)S(1)} copy(f32[128,32]{0,1:T(8,128)} %param.15) | data formatting | bytes 32768 | tf_op args[4]
  1.4 0.0 copy-start
  1.5 0.0 copy-start.1
  1.5 0.0 copy-start.2
  1.5 0.0 copy-start.3
  1.5 0.0 copy-start.4
  1.5 0.0 copy-start.5
  1.5 0.0 copy-start.6
  1.5 0.0 copy-start.7
  1.5 0.0 copy-start.8
  1.6 1.2 %copy.14.dirs_ref = f32[16,64,32]{2,1,0:T(8,128)S(1)} copy(f32[16,64,32]{1,2,0:T(8,128)} %param.16) | data formatting | bytes 262144 | tf_op args[5]
  2.8 0.0 copy-done
  2.8 0.0 copy-done.1
  2.8 0.0 copy-done.2
  2.8 0.0 copy-done.3
  2.8 0.0 copy-done.4
  2.8 0.0 copy-done.5
  2.8 0.0 copy-done.6
  2.8 0.0 copy-done.7
  2.8 0.0 copy-done.8
  2.8 52.9 %shard_map.122 = (f32[1,1,16,40]{3,2,1,0:T(8,128)S(1)}, f32[16,64,32]{2,1,0:T(8,128)S(1)}) custom-call(f32[32,128]{1,0:T(8,128)S(1)} %copy-done, f32[32,128]{1,0:T(8,128)S(1)} %copy-done.1, f32[32,128]{1,0:T(8,128)S(1)} %copy-done.2, f32[32,64]{1,0:T(8,128)S(1)} %copy-done.3, f32[128,32]{1,0:T(8,128)S(1)} %copy.13.cols_ref, ...), custom_call_target="tpu_custom_call" | custom-call | tf_op jit(solution)/shard_map/pallas_call | solution.py:521
  55.8 0.9 %copy.15 = f32[16,64,32]{1,2,0:T(8,128)} copy(f32[16,64,32]{2,1,0:T(8,128)S(1)} %get-tuple-element.3) | data formatting | bytes 262144 | tf_op jit(solution)/shard_map/pallas_call | solution.py:521
  56.7 0.6 %copy.17 = f32[1,1,16,40]{3,2,1,0:T(8,128)} copy(f32[1,1,16,40]{3,2,1,0:T(8,128)S(1)} %get-tuple-element.6) | data formatting | bytes 5120
Async XLA Ops:
  1.4 1.3 %copy-start = (f32[32,128]{1,0:T(8,128)S(1)}, f32[32,128]{1,0:T(8,128)}, u32[]{:S(2)}) copy-start(f32[32,128]{1,0:T(8,128)} %diff_ref.1) | copy-start | bytes 49156
  1.5 1.3 %copy-start.1 = (f32[32,128]{1,0:T(8,128)S(1)}, f32[32,128]{1,0:T(8,128)}, u32[]{:S(2)}) copy-start(f32[32,128]{1,0:T(8,128)} %base_ref.1) | copy-start | bytes 49156
  1.5 1.3 %copy-start.2 = (f32[32,128]{1,0:T(8,128)S(1)}, f32[32,128]{1,0:T(8,128)}, u32[]{:S(2)}) copy-start(f32[32,128]{1,0:T(8,128)} %couple_ref.1) | copy-start | bytes 49156
  1.5 1.3 %copy-start.3 = (f32[32,64]{1,0:T(8,128)S(1)}, f32[32,64]{1,0:T(8,128)}, u32[]{:S(2)}) copy-start(f32[32,64]{1,0:T(8,128)} %rows_ref.1) | copy-start | bytes 24580
  1.5 1.3 %copy-start.4 = (s32[1,1,8,8]{3,2,1,0:T(8,128)S(1)}, s32[1,1,8,8]{3,2,1,0:T(8,128)}, u32[]{:S(2)}) copy-start(s32[1,1,8,8]{3,2,1,0:T(8,128)} %cell_ref.1) | copy-start | bytes 772
  1.5 1.3 %copy-start.5 = (f32[1,1,8,8]{3,2,1,0:T(8,128)S(1)}, f32[1,1,8,8]{3,2,1,0:T(8,128)}, u32[]{:S(2)}) copy-start(f32[1,1,8,8]{3,2,1,0:T(8,128)} %weight_ref.1) | copy-start | bytes 772
  1.5 1.3 %copy-start.6 = (s32[1,1,8,8]{3,2,1,0:T(8,128)S(1)}, s32[1,1,8,8]{3,2,1,0:T(8,128)}, u32[]{:S(2)}) copy-start(s32[1,1,8,8]{3,2,1,0:T(8,128)} %gauge_ref.1) | copy-start | bytes 772
  1.5 1.3 %copy-start.7 = (s32[1,1,8]{2,1,0:T(1,128)S(1)}, s32[1,1,8]{2,1,0:T(1,128)}, u32[]{:S(2)}) copy-start(s32[1,1,8]{2,1,0:T(1,128)} %count_ref.1) | copy-start | bytes 100
  1.5 1.3 %copy-start.8 = (f32[1,1,40]{2,1,0:T(1,128)S(1)}, f32[1,1,40]{2,1,0:T(1,128)}, u32[]{:S(2)}) copy-start(f32[1,1,40]{2,1,0:T(1,128)} %prec_ref.1) | copy-start | bytes 484

commit v2 on v1

--- a/solution.py
+++ b/solution.py
@@ -13,6 +13,8 @@
 f32 = jnp.float32
 bf16 = jnp.bfloat16
 PAD = 8
+BLOCK = 2
+UNROLL = 2
 NN = (((1,), (0,)), ((), ()))
 NT = (((1,), (1,)), ((), ()))
 
@@ -70,6 +72,10 @@
     return jnp.sum(jnp.where(mine, wide, 0.0), axis=0, keepdims=True)
 
 
+def keep(ref, k, v):
+    ref[k] = jnp.broadcast_to(v[:, None, :], (v.shape[0], 8, v.shape[1]))
+
+
 def slot_of(dx, dy):
     return (dx + 1) * 3 + dy + 1
 
@@ -79,7 +85,7 @@
     diff_ref, base_ref, couple_ref, rows_ref, cols_ref, dirs_ref,
     cell_ref, weight_ref, count_ref, gauge_ref, prec_ref,
     read_ref, hess_ref,
-    pc, pt, pb, rc, rr, coef, gcoef, first_sc, pert, hum, pk, qb, rb, vr, load, grad,
+    pc, pt, pb, rc, rr, coef, gcoef, first_sc, pert, ta, ha, tb, hb, pk, qb, rb, vr, load, grad,
     proj, rsb, agb,
     near_send, near_recv, own_send, own_recv, back_send, back_recv,
     rs_send, rs_recv, ag_send, ag_recv,
@@ -88,7 +94,7 @@
     n = n_gx * n_gy
     me = gx * n_gy + gy
     height, breadth = diff_ref.shape
-    n_dirs, modes_x, modes_y = dirs_ref.shape
+    n_dirs, modes_y, modes_x = dirs_ref.shape
     peers, slots = cell_ref.shape[2], cell_ref.shape[3]
     gauges = prec_ref.shape[2]
     entries = peers * slots
@@ -136,7 +142,7 @@
         pb[k * PAD : (k + 1) * PAD, :] = ref[height - PAD :, :]
     pt[3 * PAD : 4 * PAD, :modes_x] = rows_ref[:PAD, :]
     pb[3 * PAD : 4 * PAD, :modes_x] = rows_ref[height - PAD :, :]
-    cols_t = turned(cols_ref[...])[:modes_y]
+    cols_t = cols_ref[...]
     pc[3 * height : 3 * height + modes_y, :] = cols_t
 
     pl.semaphore_wait(barrier, n - 1)
@@ -208,18 +214,18 @@
     own = (slice(PAD, PAD + height), slice(0, breadth))
     for k, (d_near, b_near) in enumerate(zip(around(diff), around(base))):
         weight = (step_ratio * 0.5) * (diff + d_near) * inside
-        coef[1 + k] = weight
+        keep(coef, 1 + k, weight)
         centre = centre - weight
         gap = 0.5 * (b_near - base)
-        gcoef[k] = (diff * gap)[own]
+        keep(gcoef, k, (diff * gap)[own])
         pull = step_ratio * gap * inside
-        coef[9 + k] = pull
+        keep(coef, 9 + k, pull)
         s_sum = s_sum + pull
-    coef[0] = centre
-    coef[5] = step_ratio * inside
-    coef[6] = couple
-    coef[7] = diff
-    coef[8] = s_sum
+    keep(coef, 0, centre)
+    keep(coef, 5, step_ratio * inside)
+    keep(coef, 6, couple)
+    keep(coef, 7, diff)
+    keep(coef, 8, s_sum)
 
     rows_ext = jnp.concatenate(
         [rr[1, 3 * PAD : 4 * PAD, :modes_x], rows_ref[...], rr[4, 3 * PAD : 4 * PAD, :modes_x]],
@@ -227,45 +233,109 @@
     )
     own_cols = slice(3 * height, 3 * height + modes_y)
     cols_ext = joined(cols_t, rc[1, own_cols, :], rc[0, own_cols, :])
-    for r in range(n_dirs):
-        first_sc[r * ext : (r + 1) * ext, :] = dot(rows_ext, dirs_ref[r])
-    pert[...] = dot(first_sc[...], cols_ext).reshape(n_dirs, ext, 2 * breadth)
-
-    def stencil(t, h, sign):
-        t_near, h_near = around(t), around(h)
-        mixed = coef[0] * h
+    group = 128 // modes_y
+    quads = n_dirs // group
+    lane_group = iota((ext, 128), 1) // modes_y
+    for q in range(quads):
+        block = dirs_ref[q * group : (q + 1) * group].reshape(128, modes_x)
+        both = dot(rows_ext, block, NT)
+        for j in range(group):
+            rows = pl.ds(q * group + j, ext, stride=n_dirs)
+            first_sc[rows, :] = jnp.where(lane_group == j, both, 0.0)
+    stacked = jnp.concatenate([cols_ext] * group, axis=0)
+    wide = (ext, n_dirs, 2 * breadth)
+
+    def perturb(i, carry):
+        rows = pl.ds(pl.multiple_of(i * 8 * n_dirs, 8 * n_dirs), 8 * n_dirs)
+        pert[pl.ds(i * 8, 8)] = dot(first_sc[rows, :], stacked).reshape((8,) + wide[1:])
+        return carry
+
+    lax.fori_loop(0, ext // 8, perturb, 0)
+
+    def sides_of(v):
+        size = v.shape[-1]
+        return pltpu.roll(v, 1, 2), pltpu.roll(v, size - 1, 2)
+
+    def near_of(ref, x, middle):
+        return (ref[pl.ds(x - 1, BLOCK)], ref[pl.ds(x + 1, BLOCK)]) + sides_of(middle)
+
+    def times(k, x, v):
+        c = coef[k, pl.ds(x, BLOCK)]
+        return jnp.concatenate(
+            [c * v[:, g * 8 : (g + 1) * 8] for g in range(n_dirs // 8)], axis=1
+        )
+
+    def over_rows(margin, body):
+        step = BLOCK * UNROLL
+        count = -(-(height + 2 * margin) // step)
+
+        def several(i, carry):
+            for u in range(UNROLL):
+                body(PAD - margin + i * step + u * BLOCK)
+            return carry
+
+        lax.fori_loop(0, count, several, 0)
+
+    def mixed_with(x, h, ref):
+        total = times(0, x, h)
+        for k, near in enumerate(near_of(ref, x, h)):
+            total = total + times(1 + k, x, near)
+        return total
+
+    def stencil(x, t_old, h_old, sign):
+        t, h = t_old[pl.ds(x, BLOCK)], h_old[pl.ds(x, BLOCK)]
         total = t
-        for k in range(4):
-            mixed = mixed + coef[1 + k] * h_near[k]
-            total = total + t_near[k]
+        for near in near_of(t_old, x, t):
+            total = total + near
+        mixed = mixed_with(x, h, h_old)
         if sign > 0:
-            return coef[5] * total + coef[6] * h, mixed - coef[6] * t
-        return coef[5] * total - coef[6] * h, mixed + coef[6] * t
-
-    def tangent(r, carry):
-        p = coef[7] * pert[r]
-        source = coef[8] * p
-        for k, p_near in enumerate(around(p)):
-            source = source + coef[9 + k] * p_near
-        t, h = coef[6] * source, coef[0] * source
-        for k, s_near in enumerate(around(source)):
-            h = h + coef[1 + k] * s_near
-        h = h + source
-        for _ in range(STEPS - 2):
-            t, h = stencil(t, h, 1)
-            h = h + source
-        hum[r] = h[own]
-        return carry
-
-    lax.fori_loop(0, n_dirs, tangent, 0)
-
-    humid = hum[...].reshape(n_dirs * height, breadth)
+            return times(5, x, total) + times(6, x, h), mixed - times(6, x, t)
+        return times(5, x, total) - times(6, x, h), mixed + times(6, x, t)
+
+    def scaled(x):
+        rows = pl.ds(x, BLOCK)
+        load[rows] = times(7, x, pert[rows])
+
+    over_rows(STEPS, scaled)
+
+    def make_source(x):
+        rows = pl.ds(x, BLOCK)
+        p = load[rows]
+        total = times(8, x, p)
+        for k, near in enumerate(near_of(load, x, p)):
+            total = total + times(9 + k, x, near)
+        pert[rows] = total
+
+    over_rows(STEPS - 1, make_source)
+
+    pairs = ((ta, ha), (tb, hb))
+
+    def first_step(x):
+        rows = pl.ds(x, BLOCK)
+        source = pert[rows]
+        ta[rows] = times(6, x, source)
+        ha[rows] = mixed_with(x, source, pert) + source
+
+    over_rows(STEPS - 2, first_step)
+    for i in range(STEPS - 2):
+        (t_old, h_old), (t_new, h_new) = pairs[i % 2], pairs[(i + 1) % 2]
+
+        def next_step(x, t_old=t_old, h_old=h_old, t_new=t_new, h_new=h_new):
+            rows = pl.ds(x, BLOCK)
+            t, h = stencil(x, t_old, h_old, 1)
+            t_new[rows] = t
+            h_new[rows] = h + pert[rows]
+
+        over_rows(STEPS - 3 - i, next_step)
+    hum = pairs[(STEPS - 2) % 2][1]
+
+    humid = hum[PAD : PAD + height, :, :breadth].reshape(height * n_dirs, breadth)
     for c in range(chunks):
         x_row, y_row, f_row = my_rows[c]
         hot = (iota((breadth, width), 0).astype(f32) == y_row).astype(f32)
-        picked = pick_dot(humid, hot).reshape(n_dirs, height, width)
-        mine = jnp.where(iota((height, width), 0).astype(f32) == x_row, f_row, 0.0)
-        picked = jnp.sum(picked * mine[None], axis=1)
+        picked = pick_dot(humid, hot).reshape(height, n_dirs, width)
+        at_x = iota(picked.shape, 0).astype(f32) == x_row[None]
+        picked = jnp.sum(jnp.where(at_x, picked, 0.0), axis=0) * f_row
         some = width // slots
         pk[c * some : (c + 1) * some] = turned(picked)[:width].reshape(some, slots, 128)
 
@@ -361,45 +431,60 @@
                 x_row, y_row, f_row = (meta_row(dx, dy, k, c) for k in range(3))
                 got = vr[dy + 1, dx + 1, c * some : (c + 1) * some].reshape(width, 128)
                 values = turned(got)[:n_dirs, :width] * f_row
-                hit_x = (iota((tall, width), 0) + first).astype(f32) == x_row
+                at_x = (iota((tall, n_dirs, width), 0) + first).astype(f32) == x_row[None]
                 y_at = iota((breadth, width), 0)
                 hit_y = y_at.astype(f32) == y_row
                 if dy:
                     hit_y = jnp.logical_and(hit_y, y_at < half if dy > 0 else y_at >= half)
-                spread_x = jnp.where(hit_x[None], values[:, None, :], 0.0)
+                spread_x = jnp.where(at_x, values[None], 0.0)
                 term = pick_dot(
-                    spread_x.reshape(n_dirs * tall, width), hit_y.astype(f32), NT
+                    spread_x.reshape(tall * n_dirs, width), hit_y.astype(f32), NT
                 )
                 tile = 1 if dy else 0
                 parts[tile] = term if parts[tile] is None else parts[tile] + term
         for tile in (0, 1):
-            load[:, at : at + tall, tile * breadth : (tile + 1) * breadth] = parts[tile].reshape(
-                n_dirs, tall, breadth
+            load[at : at + tall, :, tile * breadth : (tile + 1) * breadth] = parts[tile].reshape(
+                tall, n_dirs, breadth
             )
 
-    group = 128 // modes_y
-
-    def adjoint(r, carry):
-        b = load[r]
-        summed = b
-        a, b = -(coef[6] * b), coef[0] * b
-        for k, l_near in enumerate(around(summed)):
-            b = b + coef[1 + k] * l_near
-        summed = summed + b
-        for _ in range(STEPS - 2):
-            a, b = stencil(a, b, -1)
-            summed = summed + b
-        lam = step_ratio * summed
+    def first_back(x):
+        rows = pl.ds(x, BLOCK)
+        b = load[rows]
+        ta[rows] = -times(6, x, b)
+        b_new = mixed_with(x, b, load)
+        ha[rows] = b_new
+        pert[rows] = b + b_new
+
+    over_rows(STEPS - 1, first_back)
+    for i in range(STEPS - 2):
+        (t_old, h_old), (t_new, h_new) = pairs[i % 2], pairs[(i + 1) % 2]
+
+        def next_back(x, t_old=t_old, h_old=h_old, t_new=t_new, h_new=h_new):
+            rows = pl.ds(x, BLOCK)
+            t, h = stencil(x, t_old, h_old, -1)
+            t_new[rows] = t
+            h_new[rows] = h
+            pert[rows] = pert[rows] + h
+
+        over_rows(STEPS - 2 - i, next_back)
+
+    def gradient(x):
+        lam = pert[pl.ds(x, BLOCK)]
         total = None
-        for k, l_near in enumerate(around(lam)):
-            term = gcoef[k] * (lam[own] - l_near[own])
+        for k, near in enumerate(near_of(pert, x, lam)):
+            gap = step_ratio * (lam - near)[:, :, :breadth]
+            c = gcoef[k, pl.ds(x - PAD, BLOCK)]
+            term = jnp.concatenate(
+                [c * gap[:, g * 8 : (g + 1) * 8] for g in range(n_dirs // 8)], axis=1
+            )
             total = term if total is None else total + term
-        grad[lax.rem(r, group), r // group] = total
-        return carry
-
-    lax.fori_loop(0, n_dirs, adjoint, 0)
-
-    quads = n_dirs // group
+        start = (x - PAD) * n_dirs
+        grad[pl.ds(pl.multiple_of(start, 8), BLOCK * n_dirs), :] = total.reshape(
+            BLOCK * n_dirs, breadth
+        )
+
+    over_rows(0, gradient)
+
     half_way = None
     for j in range(group):
         pieces = []
@@ -409,7 +494,10 @@
         if j < group - 1:
             pieces.append(jnp.zeros(((group - 1 - j) * modes_y, breadth), f32))
         placed = jnp.concatenate(pieces, axis=0)
-        term = dot(grad[j].reshape(quads * height, breadth), placed, NT)
+        mine = jnp.concatenate(
+            [grad[pl.ds(q * group + j, height, stride=n_dirs), :] for q in range(quads)], axis=0
+        )
+        term = dot(mine, placed, NT)
         half_way = term if half_way is None else half_way + term
     rows_t = turned(rows_ref[...])[:modes_x, :height]
     size = proj.shape[1]
@@ -484,9 +572,11 @@
         pl.when(me >= owners)(other_part)
 
     summed = agb[...].reshape(quads, modes_x, 128)
-    for r in range(n_dirs):
-        q, j = r // group, r % group
-        hess_ref[r] = dirs_ref[r] + summed[q][:, j * modes_y : (j + 1) * modes_y]
+    for q in range(quads):
+        dirs = dirs_ref[q * group : (q + 1) * group]
+        hess_ref[q * group : (q + 1) * group] = dirs + turned(summed[q])[:, :modes_x].reshape(
+            dirs.shape
+        )
 
     for dx, dy in sides:
 
@@ -504,9 +594,12 @@
 
 
 def local(n_gx, n_gy, *args):
+    args = list(args)
+    args[4] = args[4].T
+    args[5] = args[5].transpose(0, 2, 1)
     diffusivity, dirs, cells, noise = args[0], args[5], args[6], args[10]
     height, breadth = diffusivity.shape
-    n_dirs, modes_x, modes_y = dirs.shape
+    n_dirs, modes_y, modes_x = dirs.shape
     peers, slots = cells.shape[2], cells.shape[3]
     gauges = noise.shape[2]
     n = n_gx * n_gy
@@ -514,11 +607,10 @@
     total_rows = n_dirs * modes_x * modes_y // 128
     size = max(8, total_rows // n)
     owners = total_rows // size
-    group = 128 // modes_y
     vmem = lambda *shape: pltpu.VMEM(shape, f32)
     dma = pltpu.SemaphoreType.DMA
     space = pl.BlockSpec(memory_space=pltpu.VMEM)
-    return pl.pallas_call(
+    readings, hess = pl.pallas_call(
         functools.partial(kernel, n_gx, n_gy),
         out_shape=(
             jax.ShapeDtypeStruct((1, 1, n_dirs, gauges), f32),
@@ -532,17 +624,20 @@
             vmem(5 * PAD, breadth),
             vmem(2, 3 * height + modes_y + 8, breadth),
             vmem(6, 5 * PAD, breadth),
-            vmem(13, ext, 2 * breadth),
-            vmem(4, height, breadth),
-            vmem(n_dirs * ext, modes_y),
-            vmem(n_dirs, ext, 2 * breadth),
-            vmem(n_dirs, height, breadth),
+            vmem(13, ext, 8, 2 * breadth),
+            vmem(4, height, 8, breadth),
+            vmem(ext * n_dirs, 128),
+            vmem(ext, n_dirs, 2 * breadth),
+            vmem(ext, n_dirs, 2 * breadth),
+            vmem(ext, n_dirs, 2 * breadth),
+            vmem(ext, n_dirs, 2 * breadth),
+            vmem(ext, n_dirs, 2 * breadth),
             vmem(peers, slots, 128),
             vmem(peers, slots, 128),
             vmem(peers + 2, slots, 128),
             vmem(3, 3, peers, slots, 128),
-            vmem(n_dirs, ext, 2 * breadth),
-            vmem(group, n_dirs // group, height, breadth),
+            vmem(ext, n_dirs, 2 * breadth),
+            vmem(height * n_dirs, breadth),
             vmem(owners, size, 128),
             vmem(n, size, 128),
             vmem(owners, size, 128),
@@ -561,6 +656,7 @@
             collective_id=0, has_side_effects=True, vmem_limit_bytes=40 * 1024 * 1024
         ),
     )(*args)
+    return readings, hess.transpose(0, 2, 1)
 
 
 def solution(mesh):

time: 57.5 us -> 61.8 us (1.075)
  local copies, waits for them, and re-layouts: 3.56 us -> 8.55 us
  Pallas kernels: 52.9 us -> 51.9 us
    unnamed x21 -> x24, local copies, waits for them, and re-layouts: 2.66 us -> 8.55 us
    pallas_call x1, Pallas kernels: 52.9 us -> 51.9 us  [local(): pl.pallas_call(functools.partial(kernel, n_gx, n_gy), out_shape=(jax.Shap...]
    pallas_call x1 -> x0, local copies, waits for them, and re-layouts: 0.9 us -> none  [local(): pl.pallas_call(functools.partial(kernel, n_gx, n_gy), out_shape=(jax.Shap...]
where the time goes in v2:
time: 61.8 us; the launch traced here: 61.1 us
  Pallas kernels  51.9 us (84%)
  local copies, waits for them, and re-layouts  8.55 us (14%)
  between operations  0.67 us (1%)
    pallas_call x1, Pallas kernels, local(): pl.pallas_call(functools.partial(kernel, n_gx, n_gy), out_shape=(jax.Shap...  51.9 us
    unnamed x24, local copies, waits for them, and re-layouts  8.55 us

profile of v2, /device:TPU:0, one launch (start us, length us, event | category | flops | bytes accessed | tf_op | source)
XLA Modules:
  0.0 61.1 jit_solution(9964358840773971456)
XLA Ops:
  0.6 0.0 copy-start.9
  0.6 0.0 copy-start.10
  0.7 0.6 %copy-done.9 = s32[1,1,8]{2,1,0:T(1,128)S(1)} copy-done((s32[1,1,8]{2,1,0:T(1,128)S(1)}, s32[1,1,8]{2,1,0:T(1,128)}, u32[]{:S(2)}) %copy-start.9) | copy-done | bytes 56
  1.3 0.0 copy-done.10
  1.3 0.0 copy-start
  1.3 0.9 %copy-done = f32[16,64,32]{1,2,0:T(8,128)S(1)} copy-done((f32[16,64,32]{1,2,0:T(8,128)S(1)}, f32[16,64,32]{1,2,0:T(8,128)}, u32[]{:S(2)}) %copy-start) | copy-done | bytes 131096
  2.3 0.0 copy-start.1
  2.3 0.7 %copy-done.1 = f32[32,128]{1,0:T(8,128)S(1)} copy-done((f32[32,128]{1,0:T(8,128)S(1)}, f32[32,128]{1,0:T(8,128)}, u32[]{:S(2)}) %copy-start.1) | copy-done | bytes 16408
  3.0 0.0 copy-start.2
  3.0 0.7 %copy-done.2 = f32[32,128]{1,0:T(8,128)S(1)} copy-done((f32[32,128]{1,0:T(8,128)S(1)}, f32[32,128]{1,0:T(8,128)}, u32[]{:S(2)}) %copy-start.2) | copy-done | bytes 16408
  3.7 0.0 copy-start.3
  3.7 0.7 %copy-done.3 = f32[32,128]{1,0:T(8,128)S(1)} copy-done((f32[32,128]{1,0:T(8,128)S(1)}, f32[32,128]{1,0:T(8,128)}, u32[]{:S(2)}) %copy-start.3) | copy-done | bytes 16408
  4.4 0.0 copy-start.4
  4.4 0.7 %copy-done.4 = f32[32,64]{1,0:T(8,128)S(1)} copy-done((f32[32,64]{1,0:T(8,128)S(1)}, f32[32,64]{1,0:T(8,128)}, u32[]{:S(2)}) %copy-start.4) | copy-done | bytes 8216
  5.1 0.0 copy-start.5
  5.1 0.7 %copy-done.5 = f32[128,32]{0,1:T(8,128)S(1)} copy-done((f32[128,32]{0,1:T(8,128)S(1)}, f32[128,32]{0,1:T(8,128)}, u32[]{:S(2)}) %copy-start.5) | copy-done | bytes 16408
  5.8 0.0 copy-start.6
  5.8 0.7 %copy-done.6 = s32[1,1,8,8]{3,2,1,0:T(8,128)S(1)} copy-done((s32[1,1,8,8]{3,2,1,0:T(8,128)S(1)}, s32[1,1,8,8]{3,2,1,0:T(8,128)}, u32[]{:S(2)}) %copy-start.6) | copy-done | bytes 280
  6.5 0.0 copy-start.7
  6.5 0.7 %copy-done.7 = f32[1,1,8,8]{3,2,1,0:T(8,128)S(1)} copy-done((f32[1,1,8,8]{3,2,1,0:T(8,128)S(1)}, f32[1,1,8,8]{3,2,1,0:T(8,128)}, u32[]{:S(2)}) %copy-start.7) | copy-done | bytes 280
  7.2 0.0 copy-start.8
  7.2 0.7 %copy-done.8 = s32[1,1,8,8]{3,2,1,0:T(8,128)S(1)} copy-done((s32[1,1,8,8]{3,2,1,0:T(8,128)S(1)}, s32[1,1,8,8]{3,2,1,0:T(8,128)}, u32[]{:S(2)}) %copy-start.8) | copy-done | bytes 280
  7.9 51.9 %shard_map.122 = (f32[1,1,16,40]{3,2,1,0:T(8,128)S(1)}, f32[16,32,64]{2,1,0:T(8,128)S(1)}) custom-call(f32[32,128]{1,0:T(8,128)S(1)} %copy-done.1, f32[32,128]{1,0:T(8,128)S(1)} %copy-done.2, f32[32,128]{1,0:T(8,128)S(1)} %copy-done.3, f32[32,64]{1,0:T(8,128)S(1)} %copy-done.4, f32[32,128]{1,0:T(8,128)S(1)} %bitcast.5, f32[16,32,64]{2,1,0:T(8,128)S(1)} %bitcast.3, ...), custom_call_target="tpu_custom_call" | custom-call | tf_op jit(solution)/shard_map/pallas_call | solution.py:613
  59.8 0.6 copy.15
  60.4 0.7 %copy.16 = f32[16,64,32]{1,2,0:T(8,128)} copy(f32[16,64,32]{1,2,0:T(8,128)S(1)} %bitcast.4) | data formatting | bytes 262144
Async XLA Ops:
  0.6 0.7 %copy-start.9 = (s32[1,1,8]{2,1,0:T(1,128)S(1)}, s32[1,1,8]{2,1,0:T(1,128)}, u32[]{:S(2)}) copy-start(s32[1,1,8]{2,1,0:T(1,128)} %count_ref.1) | copy-start | bytes 100
  0.6 0.7 %copy-start.10 = (f32[1,1,40]{2,1,0:T(1,128)S(1)}, f32[1,1,40]{2,1,0:T(1,128)}, u32[]{:S(2)}) copy-start(f32[1,1,40]{2,1,0:T(1,128)} %prec_ref.1) | copy-start | bytes 484
  1.3 0.9 %copy-start = (f32[16,64,32]{1,2,0:T(8,128)S(1)}, f32[16,64,32]{1,2,0:T(8,128)}, u32[]{:S(2)}) copy-start(f32[16,64,32]{1,2,0:T(8,128)} %param.16) | copy-start | bytes 393220
  2.3 0.7 %copy-start.1 = (f32[32,128]{1,0:T(8,128)S(1)}, f32[32,128]{1,0:T(8,128)}, u32[]{:S(2)}) copy-start(f32[32,128]{1,0:T(8,128)} %diff_ref.1) | copy-start | bytes 49156
  3.0 0.7 %copy-start.2 = (f32[32,128]{1,0:T(8,128)S(1)}, f32[32,128]{1,0:T(8,128)}, u32[]{:S(2)}) copy-start(f32[32,128]{1,0:T(8,128)} %base_ref.1) | copy-start | bytes 49156
  3.7 0.7 %copy-start.3 = (f32[32,128]{1,0:T(8,128)S(1)}, f32[32,128]{1,0:T(8,128)}, u32[]{:S(2)}) copy-start(f32[32,128]{1,0:T(8,128)} %couple_ref.1) | copy-start | bytes 49156
  4.4 0.7 %copy-start.4 = (f32[32,64]{1,0:T(8,128)S(1)}, f32[32,64]{1,0:T(8,128)}, u32[]{:S(2)}) copy-start(f32[32,64]{1,0:T(8,128)} %rows_ref.1) | copy-start | bytes 24580
  5.1 0.7 %copy-start.5 = (f32[128,32]{0,1:T(8,128)S(1)}, f32[128,32]{0,1:T(8,128)}, u32[]{:S(2)}) copy-start(f32[128,32]{0,1:T(8,128)} %param.15) | copy-start | bytes 49156
  5.8 0.7 %copy-start.6 = (s32[1,1,8,8]{3,2,1,0:T(8,128)S(1)}, s32[1,1,8,8]{3,2,1,0:T(8,128)}, u32[]{:S(2)}) copy-start(s32[1,1,8,8]{3,2,1,0:T(8,128)} %cell_ref.1) | copy-start | bytes 772
  6.5 0.7 %copy-start.7 = (f32[1,1,8,8]{3,2,1,0:T(8,128)S(1)}, f32[1,1,8,8]{3,2,1,0:T(8,128)}, u32[]{:S(2)}) copy-start(f32[1,1,8,8]{3,2,1,0:T(8,128)} %weight_ref.1) | copy-start | bytes 772
  7.2 0.7 %copy-start.8 = (s32[1,1,8,8]{3,2,1,0:T(8,128)S(1)}, s32[1,1,8,8]{3,2,1,0:T(8,128)}, u32[]{:S(2)}) copy-start(s32[1,1,8,8]{3,2,1,0:T(8,128)} %gauge_ref.1) | copy-start | bytes 772

commit v3 on v2

--- a/solution.py
+++ b/solution.py
@@ -13,8 +13,8 @@
 f32 = jnp.float32
 bf16 = jnp.bfloat16
 PAD = 8
+N_IN = 11
 BLOCK = 2
-UNROLL = 2
 NN = (((1,), (0,)), ((), ()))
 NT = (((1,), (1,)), ((), ()))
 
@@ -82,6 +82,21 @@
 
 def kernel(
     n_gx, n_gy,
+    *refs,
+):
+    inputs, outputs = refs[:N_IN], refs[N_IN : N_IN + 2]
+    held, rest = refs[N_IN + 2 : 2 * N_IN + 2], refs[2 * N_IN + 2 :]
+    copies = [
+        pltpu.make_async_copy(src, dst, rest[-1].at[k])
+        for k, (src, dst) in enumerate(zip(inputs, held))
+    ]
+    for copy in copies:
+        copy.start()
+    work(n_gx, n_gy, copies, *held, *outputs, *rest[:-1])
+
+
+def work(
+    n_gx, n_gy, copies,
     diff_ref, base_ref, couple_ref, rows_ref, cols_ref, dirs_ref,
     cell_ref, weight_ref, count_ref, gauge_ref, prec_ref,
     read_ref, hess_ref,
@@ -119,6 +134,9 @@
         return carry
 
     lax.fori_loop(1, n, greet, 0)
+
+    for copy in copies:
+        copy.wait()
 
     live = iota((peers, slots), 1).astype(f32) < column(count_ref[0].astype(f32))
     factor = jnp.where(live, weight_ref[0, 0], 0.0)
@@ -180,8 +198,6 @@
         @pl.when(exists(dx, dy))
         def _(dx=dx, dy=dy):
             near_copy(-dx, -dy).wait_recv()
-
-    lane = iota((ext, breadth), 1)
 
     def joined(middle, right, left):
         return jnp.concatenate([middle, jnp.where(iota(right.shape, 1) < half, right, left)], axis=1)
@@ -247,7 +263,10 @@
 
     def perturb(i, carry):
         rows = pl.ds(pl.multiple_of(i * 8 * n_dirs, 8 * n_dirs), 8 * n_dirs)
-        pert[pl.ds(i * 8, 8)] = dot(first_sc[rows, :], stacked).reshape((8,) + wide[1:])
+        p = dot(first_sc[rows, :], stacked).reshape((8,) + wide[1:])
+        c = coef[7, pl.ds(i * 8, 8)]
+        for g in range(0, n_dirs, 8):
+            load[pl.ds(i * 8, 8), g : g + 8, :] = c * p[:, g : g + 8]
         return carry
 
     lax.fori_loop(0, ext // 8, perturb, 0)
@@ -266,15 +285,18 @@
         )
 
     def over_rows(margin, body):
-        step = BLOCK * UNROLL
-        count = -(-(height + 2 * margin) // step)
+        blocks = (height + 2 * margin) // BLOCK
+        unroll = next((u for u in (8, 7, 6, 5) if blocks % u == 0), 0)
+        if not unroll:
+            blocks += 1
+            unroll = next(u for u in (6, 5, 8, 7) if blocks % u == 0)
 
         def several(i, carry):
-            for u in range(UNROLL):
-                body(PAD - margin + i * step + u * BLOCK)
+            for u in range(unroll):
+                body(PAD - margin + (i * unroll + u) * BLOCK)
             return carry
 
-        lax.fori_loop(0, count, several, 0)
+        lax.fori_loop(0, blocks // unroll, several, 0)
 
     def mixed_with(x, h, ref):
         total = times(0, x, h)
@@ -291,12 +313,6 @@
         if sign > 0:
             return times(5, x, total) + times(6, x, h), mixed - times(6, x, t)
         return times(5, x, total) - times(6, x, h), mixed + times(6, x, t)
-
-    def scaled(x):
-        rows = pl.ds(x, BLOCK)
-        load[rows] = times(7, x, pert[rows])
-
-    over_rows(STEPS, scaled)
 
     def make_source(x):
         rows = pl.ds(x, BLOCK)
@@ -616,9 +632,10 @@
             jax.ShapeDtypeStruct((1, 1, n_dirs, gauges), f32),
             jax.ShapeDtypeStruct(dirs.shape, f32),
         ),
-        in_specs=[space] * len(args),
+        in_specs=[pl.BlockSpec(memory_space=pltpu.HBM)] * len(args),
         out_specs=(space, space),
-        scratch_shapes=[
+        scratch_shapes=[pltpu.VMEM(a.shape, a.dtype) for a in args]
+        + [
             vmem(3 * height + modes_y + 8, breadth),
             vmem(5 * PAD, breadth),
             vmem(5 * PAD, breadth),
@@ -651,6 +668,7 @@
             dma,
             dma,
             dma,
+            dma((N_IN,)),
         ],
         compiler_params=pltpu.CompilerParams(
             collective_id=0, has_side_effects=True, vmem_limit_bytes=40 * 1024 * 1024

time: 61.8 us -> 56.1 us (0.908)
  Pallas kernels: 51.9 us -> 46.1 us
    pallas_call x1, Pallas kernels: 51.9 us -> 46.1 us  [local(): pl.pallas_call(functools.partial(kernel, n_gx, n_gy), out_shape=(jax.Shap...]
where the time goes in v3:
time: 56.1 us; the launch traced here: 55.4 us
  Pallas kernels  46.1 us (82%)
  local copies, waits for them, and re-layouts  8.55 us (15%)
  between operations  0.67 us (1%)
    pallas_call x1, Pallas kernels, local(): pl.pallas_call(functools.partial(kernel, n_gx, n_gy), out_shape=(jax.Shap...  46.1 us
    unnamed x24, local copies, waits for them, and re-layouts  8.55 us

profile of v3, /device:TPU:0, one launch (start us, length us, event | category | flops | bytes accessed | tf_op | source)
XLA Modules:
  0.0 55.4 jit_solution(11239694612122789988)
XLA Ops:
  0.6 0.0 copy-start.9
  0.6 0.0 copy-start.10
  0.7 0.6 %copy-done.9 = s32[1,1,8]{2,1,0:T(1,128)S(1)} copy-done((s32[1,1,8]{2,1,0:T(1,128)S(1)}, s32[1,1,8]{2,1,0:T(1,128)}, u32[]{:S(2)}) %copy-start.9) | copy-done | bytes 56
  1.3 0.0 copy-done.10
  1.3 0.0 copy-start
  1.3 0.9 %copy-done = f32[16,64,32]{1,2,0:T(8,128)S(1)} copy-done((f32[16,64,32]{1,2,0:T(8,128)S(1)}, f32[16,64,32]{1,2,0:T(8,128)}, u32[]{:S(2)}) %copy-start) | copy-done | bytes 131096
  2.3 0.0 copy-start.1
  2.3 0.7 %copy-done.1 = f32[32,128]{1,0:T(8,128)S(1)} copy-done((f32[32,128]{1,0:T(8,128)S(1)}, f32[32,128]{1,0:T(8,128)}, u32[]{:S(2)}) %copy-start.1) | copy-done | bytes 16408
  3.0 0.0 copy-start.2
  3.0 0.7 %copy-done.2 = f32[32,128]{1,0:T(8,128)S(1)} copy-done((f32[32,128]{1,0:T(8,128)S(1)}, f32[32,128]{1,0:T(8,128)}, u32[]{:S(2)}) %copy-start.2) | copy-done | bytes 16408
  3.7 0.0 copy-start.3
  3.7 0.7 %copy-done.3 = f32[32,128]{1,0:T(8,128)S(1)} copy-done((f32[32,128]{1,0:T(8,128)S(1)}, f32[32,128]{1,0:T(8,128)}, u32[]{:S(2)}) %copy-start.3) | copy-done | bytes 16408
  4.4 0.0 copy-start.4
  4.4 0.7 %copy-done.4 = f32[32,64]{1,0:T(8,128)S(1)} copy-done((f32[32,64]{1,0:T(8,128)S(1)}, f32[32,64]{1,0:T(8,128)}, u32[]{:S(2)}) %copy-start.4) | copy-done | bytes 8216
  5.1 0.0 copy-start.5
  5.1 0.7 %copy-done.5 = f32[128,32]{0,1:T(8,128)S(1)} copy-done((f32[128,32]{0,1:T(8,128)S(1)}, f32[128,32]{0,1:T(8,128)}, u32[]{:S(2)}) %copy-start.5) | copy-done | bytes 16408
  5.8 0.0 copy-start.6
  5.8 0.7 %copy-done.6 = s32[1,1,8,8]{3,2,1,0:T(8,128)S(1)} copy-done((s32[1,1,8,8]{3,2,1,0:T(8,128)S(1)}, s32[1,1,8,8]{3,2,1,0:T(8,128)}, u32[]{:S(2)}) %copy-start.6) | copy-done | bytes 280
  6.5 0.0 copy-start.7
  6.5 0.7 %copy-done.7 = f32[1,1,8,8]{3,2,1,0:T(8,128)S(1)} copy-done((f32[1,1,8,8]{3,2,1,0:T(8,128)S(1)}, f32[1,1,8,8]{3,2,1,0:T(8,128)}, u32[]{:S(2)}) %copy-start.7) | copy-done | bytes 280
  7.2 0.0 copy-start.8
  7.2 0.7 %copy-done.8 = s32[1,1,8,8]{3,2,1,0:T(8,128)S(1)} copy-done((s32[1,1,8,8]{3,2,1,0:T(8,128)S(1)}, s32[1,1,8,8]{3,2,1,0:T(8,128)}, u32[]{:S(2)}) %copy-start.8) | copy-done | bytes 280
  7.9 46.1 %shard_map.122 = (f32[1,1,16,40]{3,2,1,0:T(8,128)S(1)}, f32[16,32,64]{2,1,0:T(8,128)S(1)}) custom-call(f32[32,128]{1,0:T(8,128)S(1)} %copy-done.1, f32[32,128]{1,0:T(8,128)S(1)} %copy-done.2, f32[32,128]{1,0:T(8,128)S(1)} %copy-done.3, f32[32,64]{1,0:T(8,128)S(1)} %copy-done.4, f32[32,128]{1,0:T(8,128)S(1)} %bitcast.5, f32[16,32,64]{2,1,0:T(8,128)S(1)} %bitcast.3, ...), custom_call_target="tpu_custom_call" | custom-call | tf_op jit(solution)/shard_map/pallas_call | solution.py:629
  54.0 0.6 %copy.15 = f32[1,1,16,40]{3,2,1,0:T(8,128)} copy(f32[1,1,16,40]{3,2,1,0:T(8,128)S(1)} %get-tuple-element.8) | data formatting | bytes 5120
  54.6 0.7 %copy.16 = f32[16,64,32]{1,2,0:T(8,128)} copy(f32[16,64,32]{1,2,0:T(8,128)S(1)} %bitcast.4) | data formatting | bytes 262144
Async XLA Ops:
  0.6 0.7 %copy-start.9 = (s32[1,1,8]{2,1,0:T(1,128)S(1)}, s32[1,1,8]{2,1,0:T(1,128)}, u32[]{:S(2)}) copy-start(s32[1,1,8]{2,1,0:T(1,128)} %refs_8_.1) | copy-start | bytes 100
  0.6 0.7 %copy-start.10 = (f32[1,1,40]{2,1,0:T(1,128)S(1)}, f32[1,1,40]{2,1,0:T(1,128)}, u32[]{:S(2)}) copy-start(f32[1,1,40]{2,1,0:T(1,128)} %refs_10_.1) | copy-start | bytes 484
  1.3 0.9 %copy-start = (f32[16,64,32]{1,2,0:T(8,128)S(1)}, f32[16,64,32]{1,2,0:T(8,128)}, u32[]{:S(2)}) copy-start(f32[16,64,32]{1,2,0:T(8,128)} %param.16) | copy-start | bytes 393220
  2.3 0.7 %copy-start.1 = (f32[32,128]{1,0:T(8,128)S(1)}, f32[32,128]{1,0:T(8,128)}, u32[]{:S(2)}) copy-start(f32[32,128]{1,0:T(8,128)} %refs_0_.1) | copy-start | bytes 49156
  3.0 0.7 %copy-start.2 = (f32[32,128]{1,0:T(8,128)S(1)}, f32[32,128]{1,0:T(8,128)}, u32[]{:S(2)}) copy-start(f32[32,128]{1,0:T(8,128)} %refs_1_.1) | copy-start | bytes 49156
  3.7 0.7 %copy-start.3 = (f32[32,128]{1,0:T(8,128)S(1)}, f32[32,128]{1,0:T(8,128)}, u32[]{:S(2)}) copy-start(f32[32,128]{1,0:T(8,128)} %refs_2_.1) | copy-start | bytes 49156
  4.4 0.7 %copy-start.4 = (f32[32,64]{1,0:T(8,128)S(1)}, f32[32,64]{1,0:T(8,128)}, u32[]{:S(2)}) copy-start(f32[32,64]{1,0:T(8,128)} %refs_3_.1) | copy-start | bytes 24580
  5.1 0.7 %copy-start.5 = (f32[128,32]{0,1:T(8,128)S(1)}, f32[128,32]{0,1:T(8,128)}, u32[]{:S(2)}) copy-start(f32[128,32]{0,1:T(8,128)} %param.15) | copy-start | bytes 49156
  5.8 0.7 %copy-start.6 = (s32[1,1,8,8]{3,2,1,0:T(8,128)S(1)}, s32[1,1,8,8]{3,2,1,0:T(8,128)}, u32[]{:S(2)}) copy-start(s32[1,1,8,8]{3,2,1,0:T(8,128)} %refs_6_.1) | copy-start | bytes 772
  6.5 0.7 %copy-start.7 = (f32[1,1,8,8]{3,2,1,0:T(8,128)S(1)}, f32[1,1,8,8]{3,2,1,0:T(8,128)}, u32[]{:S(2)}) copy-start(f32[1,1,8,8]{3,2,1,0:T(8,128)} %refs_7_.1) | copy-start | bytes 772
  7.2 0.7 %copy-start.8 = (s32[1,1,8,8]{3,2,1,0:T(8,128)S(1)}, s32[1,1,8,8]{3,2,1,0:T(8,128)}, u32[]{:S(2)}) copy-start(s32[1,1,8,8]{3,2,1,0:T(8,128)} %refs_9_.1) | copy-start | bytes 772
